TPU v7x, 256 devices: a whole 4x4x8 slice. The times are simulated.
256 devices in a mesh: fsdp: 64 (over x, z, y_lo), tile: 4 (over y_hi, core).
Axes of the slice: x: 4, y: 4 (y_hi: 2, y_lo: 2; y = y_hi * 2 + y_lo), z: 8, core: 2. Of those that a mesh axis runs over, the one named last changes fastest.
Arguments:
- tokens: bfloat16 [65536, 1536], P('fsdp', 'tile'), may hold values from -6 to 6
- ln_gain: float32 [1536], replicated, may hold values from 0.25 to 1.75
- w_up: bfloat16 [1536, 6144], P('fsdp', 'tile'), may hold values from -0.15625 to 0.15625
- w_down: bfloat16 [6144, 1536], P('tile', 'fsdp'), may hold values from -0.078125 to 0.078125
- w_flux_in: bfloat16 [1536, 768], P('tile'), may hold values from -0.15625 to 0.15625
- w_flux_out: bfloat16 [768, 128], replicated, may hold values from -0.21875 to 0.21875
- ocean_state: bfloat16 [2048, 128, 256], P('fsdp', 'tile'), may hold values from -6 to 6
- land_mask: int32 [2048, 128], P('fsdp', 'tile'), may hold values from 0 to 1, as said below
- column_map: int32 [2048, 128], P('fsdp', 'tile'), may hold values from 0 to 65535, as said below
- w_couple: bfloat16 [128, 256], replicated, may hold values from -0.5 to 0.5
- dw_kernel: float32 [2, 7, 7, 256], replicated, may hold values from -0.875 to 0.875
- ocean_gain: float32 [2, 256], replicated, may hold values from 0.25 to 1.75
- w_pw1: bfloat16 [2, 256, 1024], replicated, may hold values from -0.375 to 0.375
- w_pw2: bfloat16 [2, 1024, 256], replicated, may hold values from -0.1875 to 0.1875
Outputs:
- atm_out: bfloat16 [65536, 1536], P('fsdp', 'tile')
- ocean_out: bfloat16 [2048, 128, 256], P('fsdp', 'tile')
Inputs may be any that keep to these rules, and one draw needn't show every extreme that they name: `land_mask`: 0 or 1; land comes in regions of 8 x 8 cells whose ocean share varies. `column_map`: the column in grid row x names a token between (x // 32) * 1024 - 256 and (x // 32 + 1) * 1024 + 255.
All inputs are finite; a program needn't handle non-finite values.
Results may differ from a plain program's by a relative error of at most 0.014.
Values may be sent and summed in bfloat16 or wider, within the bound.
A program may use at most 128 MiB of HBM per device.

v0:
```python
import jax
import jax.numpy as jnp
from jax import lax
from jax.sharding import PartitionSpec as P


def with_halo(block, sides, width):
    for axis, dim in sides:
        count = lax.axis_size(axis)
        forward = [(i, i + 1) for i in range(count - 1)]
        backward = [(target, source) for source, target in forward]
        low = lax.ppermute(
            lax.slice_in_dim(block, block.shape[dim] - width, None, axis=dim), axis, forward
        )
        high = lax.ppermute(lax.slice_in_dim(block, 0, width, axis=dim), axis, backward)
        block = jnp.concatenate([low, block, high], axis=dim)
    return block


def layer_norm(values, gain):
    center = values - jnp.mean(values, axis=-1, keepdims=True)
    spread = jnp.mean(center * center, axis=-1, keepdims=True)
    return center * lax.rsqrt(spread + 1e-06) * gain


def conv_block(padded, region_mask, kernel, gain, w_one, w_two):
    rows = padded.shape[0] - 6
    cols = padded.shape[1] - 6
    chans = padded.shape[2]
    total = jnp.zeros((rows, cols, chans), jnp.float32)
    for first in range(7):
        for second in range(7):
            total = (
                total
                + padded[first : first + rows, second : second + cols].astype(jnp.float32)
                * kernel[first, second]
            )
    pnorm = layer_norm(total, gain).astype(jnp.bfloat16).reshape(rows * cols, chans)
    inner = jax.nn.gelu(
        jnp.dot(pnorm, w_one, preferred_element_type=jnp.float32), approximate=True
    ).astype(jnp.bfloat16)
    lowered = jnp.dot(inner, w_two, preferred_element_type=jnp.float32).reshape(rows, cols, chans)
    before = padded[3 : 3 + rows, 3 : 3 + cols].astype(jnp.float32)
    return (region_mask[..., None] * (before + lowered)).astype(jnp.bfloat16)


def body(
    tokens,
    ln_gain,
    w_up,
    w_down,
    w_flux_in,
    w_flux_out,
    ocean_state,
    land_mask,
    column_map,
    w_couple,
    dw_kernel,
    ocean_gain,
    w_pw1,
    w_pw2,
):
    band_rows = tokens.shape[0]
    whole = lax.all_gather(tokens, "tile", axis=1, tiled=True)
    normed = layer_norm(whole.astype(jnp.float32), ln_gain).astype(jnp.bfloat16)
    up_whole = lax.all_gather(w_up, "fsdp", axis=0, tiled=True)
    pre = jnp.dot(normed, up_whole, preferred_element_type=jnp.float32)
    hidden = jax.nn.gelu(pre, approximate=True).astype(jnp.bfloat16)
    down_whole = lax.all_gather(w_down, "fsdp", axis=1, tiled=True)
    terms = jnp.dot(hidden, down_whole, preferred_element_type=jnp.float32)
    delta = lax.psum_scatter(terms, "tile", scatter_dimension=1, tiled=True)
    atm_out = (tokens.astype(jnp.float32) + delta).astype(jnp.bfloat16)
    flux_pre = lax.psum(jnp.dot(atm_out, w_flux_in, preferred_element_type=jnp.float32), "tile")
    flux_hidden = jax.nn.gelu(flux_pre, approximate=True).astype(jnp.bfloat16)
    fluxes = jnp.dot(flux_hidden, w_flux_out, preferred_element_type=jnp.float32).astype(
        jnp.bfloat16
    )
    rim_rows = band_rows // 4
    window = with_halo(fluxes, (("fsdp", 0),), rim_rows)
    band = lax.axis_index("fsdp")
    local_index = (column_map - (band * band_rows - rim_rows)).reshape(-1)
    picked = jnp.take(window, local_index, axis=0)
    grid_rows = ocean_state.shape[0]
    grid_cols = ocean_state.shape[1]
    chans = ocean_state.shape[2]
    forcing = jnp.dot(picked, w_couple, preferred_element_type=jnp.float32).reshape(
        grid_rows, grid_cols, chans
    )
    mask = land_mask.astype(jnp.float32)
    state = (mask[..., None] * (ocean_state.astype(jnp.float32) + forcing)).astype(jnp.bfloat16)
    count = dw_kernel.shape[0]
    for block in range(count):
        padded = with_halo(state, (("fsdp", 0), ("tile", 1)), 3)
        state = conv_block(
            padded, mask, dw_kernel[block], ocean_gain[block], w_pw1[block], w_pw2[block]
        )
    return (atm_out, state)


def solution(mesh):
    placed = (
        P("fsdp", "tile"),
        P(),
        P("fsdp", "tile"),
        P("tile", "fsdp"),
        P("tile", None),
        P(),
        P("fsdp", "tile", None),
        P("fsdp", "tile"),
        P("fsdp", "tile"),
        P(),
        P(),
        P(),
        P(),
        P(),
    )
    return jax.shard_map(
        body,
        mesh=mesh,
        in_specs=placed,
        out_specs=(P("fsdp", "tile"), P("fsdp", "tile", None)),
        check_vma=False,
    )
```

profile of v0, /device:TPU:1, one launch (start us, length us, event | category | flops | bytes accessed | tf_op | source)
XLA Modules:
  0.0 919.2 jit_solution(5960225791835715964)
XLA Ops:
  7.2 0.0 copy-start
  7.2 0.0 all-gather.4.cloned.1.call-start
  7.2 0.7 all-gather.4.cloned.1.call-update
  7.9 0.0 all-gather.6.cloned.1.call-start
  8.0 0.7 all-gather.6.cloned.1.call-update
  8.7 0.0 all-gather.8.cloned.1.call-start
  8.7 0.7 all-gather.8.cloned.1.call-update
  9.4 0.0 reduce-scatter.2.cloned.1.call-start
  9.5 39.7 %all-gather.4.cloned.1.call-done = bf16[1024,1536]{1,0:T(8,128)(2,1)} async-done(((bf16[1024,384]{1,0:T(8,128)(2,1)}), bf16[1024,1536]{1,0:T(8,128)(2,1)}) %all-gather.4.cloned.1.call-update) | async-done | bytes 3145744 | tf_op jit(solution)/shard_map/all_gather | solution.py:64
  49.2 2.5 convert_reduce_fusion
  51.7 0.3 copy-done.1
  52.0 1.0 fusion.2
  53.0 258.8 %all-gather.6.cloned.1.call-done = bf16[1536,1536]{1,0:T(8,128)(2,1)} async-done(((bf16[24,1536]{1,0:T(8,128)(2,1)}), bf16[1536,1536]{1,0:T(8,128)(2,1)}) %all-gather.6.cloned.1.call-update) | async-done | bytes 4718608 | tf_op jit(solution)/shard_map/all_gather | solution.py:66
  311.8 304.7 %all-gather.8.cloned.1.call-done = bf16[1536,1536]{0,1:T(8,128)(2,1)} async-done(((bf16[1536,24]{0,1:T(8,128)(2,1)}), bf16[1536,1536]{0,1:T(8,128)(2,1)}) %all-gather.8.cloned.1.call-update) | async-done | bytes 4718608 | tf_op jit(solution)/shard_map/all_gather | solution.py:69
  616.5 17.4 %fusion.37 = f32[1024,1536]{1,0:T(8,128)} fusion(bf16[1536,1536]{0,1:T(8,128)(2,1)} %all-gather.8.cloned.1.call-done, bf16[1536,1536]{1,0:T(8,128)(2,1)} %all-gather.6.cloned.1.call-done, bf16[1024,1536]{1,0:T(8,128)(2,1)} %all-gather.4.cloned.1.call-done, f32[1536]{0:T(1024)S(1)} %copy-done.13, f32[1024]{0:T(1024)S(1)} %add_rsqrt_fusion.2, ...), kind=kOutput, calls=%fused_computation.44 | convolution fusion | flops 9685696512 | bytes 18888704 | tf_op jit(solution)/shard_map/dot_general | solution.py:70
  633.9 0.0 reduce-scatter.2.cloned.1.call-update
  633.9 0.0 all-reduce.2.cloned.1.call-start
  633.9 111.6 %reduce-scatter.2.cloned.1.call-done = f32[1024,384]{1,0:T(8,128)} async-done(((f32[1024,1536]{1,0:T(8,128)}), f32[1024,384]{1,0:T(8,128)}) %reduce-scatter.2.cloned.1.call-update) | async-done | bytes 1572880 | tf_op jit(solution)/shard_map/reduce_scatter | solution.py:71
  745.6 1.6 add_convert_fusion
  747.2 0.0 copy-start.3
  747.2 0.0 copy-start.7
  747.2 0.0 copy-start.5
  747.2 0.0 copy-start.12
  747.3 2.7 fusion.155
  749.9 0.0 all-reduce.2.cloned.1.call-update
  750.0 0.1 reshape.97
  750.1 0.1 reshape.96
  750.2 0.1 fusion.147
  750.4 80.6 %all-reduce.2.cloned.1.call-done = f32[1024,768]{1,0:T(8,128)} async-done(((f32[1024,768]{1,0:T(8,128)}), f32[1024,768]{1,0:T(8,128)}) %all-reduce.2.cloned.1.call-update) | async-done | bytes 3145744 | tf_op jit(solution)/shard_map/psum | solution.py:73
  830.9 3.0 fusion.58
  834.0 0.0 copy-start.6
  834.0 2.3 collective-permute-start
  836.4 1.5 collective-permute-start.1
  837.9 4.2 collective-permute-done.1
  842.1 0.0 copy-start.9
  842.1 3.2 gather_fusion
  845.3 0.4 fusion.127
  845.7 0.2 multiply_convert_fusion.2
  846.0 4.3 collective-permute-start.2
  850.2 1.3 collective-permute-start.3
  851.6 3.5 collective-permute-done.3
  855.1 0.1 pad_maximum_fusion.12
  855.1 5.2 collective-permute-start.4
  860.3 1.9 collective-permute-start.5
  862.3 5.3 collective-permute-done.5
  867.6 0.5 maximum_maximum_fusion
  868.1 9.1 fusion.142
  877.2 0.4 multiply_reduce_fusion.1
  877.6 0.3 multiply_convert_fusion.1
  878.0 1.5 fusion.20
  879.5 0.7 fusion.56
  880.2 3.1 collective-permute-start.6
  883.3 1.3 collective-permute-start.7
  884.7 3.5 collective-permute-done.7
  888.2 0.1 pad_maximum_fusion.9
  888.2 3.9 collective-permute-start.8
  892.1 2.1 collective-permute-start.9
  894.3 5.0 collective-permute-done.9
  899.3 0.5 maximum_maximum_fusion.1
  899.8 9.1 fusion.140
  909.0 0.4 multiply_reduce_fusion
  909.4 0.3 multiply_convert_fusion
  909.7 1.5 fusion.28
  911.2 1.5 fusion.57
  (48 shorter events, 0.3 us)
Async XLA Ops:
  7.2 740.0 %copy-start = (bf16[384,768]{1,0:T(8,128)(2,1)S(1)}, bf16[384,768]{1,0:T(8,128)(2,1)}, u32[]{:S(2)}) copy-start(bf16[384,768]{1,0:T(8,128)(2,1)} %param.18) | copy-start | bytes 1769476
  7.2 42.0 %all-gather.4.cloned.1.call-start = ((), (), s32[]{:S(2)}) async-start(), calls=%async_computation.1 | async-start | bytes 3932160 | tf_op jit(solution)/shard_map/all_gather | solution.py:64
  7.9 303.9 %all-gather.6.cloned.1.call-start = ((), (), s32[]{:S(2)}) async-start(), calls=%async_computation.2 | async-start | bytes 4792320 | tf_op jit(solution)/shard_map/all_gather | solution.py:66
  8.7 607.8 %all-gather.8.cloned.1.call-start = ((), (), s32[]{:S(2)}) async-start(), calls=%async_computation.3 | async-start | bytes 4792320 | tf_op jit(solution)/shard_map/all_gather | solution.py:69
  9.4 607.1 %copy-start.13 = (f32[1536]{0:T(1024)S(1)}, f32[1536]{0:T(1024)}, u32[]{:S(2)}) copy-start(f32[1536]{0:T(1024)} %param.15) | copy-start | bytes 18436
  9.4 736.2 %reduce-scatter.2.cloned.1.call-start = ((), (), s32[]{:S(2)}) async-start(), calls=%async_computation.4 | async-start | bytes 7864320 | tf_op jit(solution)/shard_map/reduce_scatter | solution.py:71
  49.2 2.8 copy-start.1
  633.9 111.7 %copy-start.2 = (bf16[1024,384]{1,0:T(8,128)(2,1)S(1)}, bf16[1024,384]{1,0:T(8,128)(2,1)}, u32[]{:S(2)}) copy-start(bf16[1024,384]{1,0:T(8,128)(2,1)} %param.14) | copy-start | bytes 2359300
  633.9 197.0 %all-reduce.2.cloned.1.call-start = ((), (), s32[]{:S(2)}) async-start(), calls=%async_computation.5 | async-start | bytes 6291456 | tf_op jit(solution)/shard_map/psum | solution.py:73
  747.2 2.7 copy-start.3
  747.2 2.8 copy-start.7
  747.2 2.9 copy-start.5
  747.2 83.7 %copy-start.12 = (bf16[768,128]{1,0:T(8,128)(2,1)S(1)}, bf16[768,128]{1,0:T(8,128)(2,1)}, u32[]{:S(2)}) copy-start(bf16[768,128]{1,0:T(8,128)(2,1)} %param.19) | copy-start | bytes 589828
  750.4 87.5 %copy-start.8 = (s32[32,32]{1,0:T(8,128)S(1)}, s32[32,32]{1,0:T(8,128)}, u32[]{:S(2)}) copy-start(s32[32,32]{1,0:T(8,128)} %param.21) | copy-start | bytes 12292
  834.0 11.4 %copy-start.6 = (bf16[128,256]{1,0:T(8,128)(2,1)S(1)}, bf16[128,256]{1,0:T(8,128)(2,1)}, u32[]{:S(2)}) copy-start(bf16[128,256]{1,0:T(8,128)(2,1)} %param.23) | copy-start | bytes 196612
  834.0 11.7 %copy-start.4 = (bf16[32,32,256]{2,1,0:T(8,128)(2,1)S(1)}, bf16[32,32,256]{2,1,0:T(8,128)(2,1)}, u32[]{:S(2)}) copy-start(bf16[32,32,256]{2,1,0:T(8,128)(2,1)} %param.20) | copy-start | bytes 1572868
  834.0 3.9 collective-permute-start
  836.4 5.7 collective-permute-start.1
  842.1 20.2 %copy-start.9 = (f32[2,256]{1,0:T(2,128)S(1)}, f32[2,256]{1,0:T(2,128)}, u32[]{:S(2)}) copy-start(f32[2,256]{1,0:T(2,128)} %param.25) | copy-start | bytes 6148
  846.0 5.6 collective-permute-start.2
  850.2 4.8 collective-permute-start.3
  855.1 7.2 collective-permute-start.4
  860.3 7.2 collective-permute-start.5
  868.1 9.9 %copy-start.10 = (bf16[2,256,1024]{2,1,0:T(8,128)(2,1)S(1)}, bf16[2,256,1024]{2,1,0:T(8,128)(2,1)}, u32[]{:S(2)}) copy-start(bf16[2,256,1024]{2,1,0:T(8,128)(2,1)} %param.26) | copy-start | bytes 3145732
  878.0 1.5 copy-start.11
  880.2 4.4 collective-permute-start.6
  883.3 4.8 collective-permute-start.7
  888.2 6.1 collective-permute-start.8
  892.1 7.2 collective-permute-start.9
Sparse Core Ops, SparseCore 0:
  9.8 39.2 all-gather.3
  51.0 260.7 all-gather.5
  313.6 302.8 all-gather.7
  634.0 111.5 reduce-scatter.1
  750.1 80.8 all-reduce.1
where the time goes:
time: 922 us; the launch traced here: 919 us
  waiting for transfers between devices  819 us (89%)
  matrix products  28.6 us (3%)
  starting transfers between devices  27.1 us (3%)
  other arithmetic  26.2 us (3%)
  between operations  14.3 us (2%)
    all_gather x1, waiting for transfers between devices, body(): down_whole = lax.all_gather(w_down, 'fsdp', axis=1, tiled=True)  305 us
    all_gather x1, waiting for transfers between devices, body(): up_whole = lax.all_gather(w_up, 'fsdp', axis=0, tiled=True)  259 us
    reduce_scatter x1, waiting for transfers between devices, body(): delta = lax.psum_scatter(terms, 'tile', scatter_dimension=1, tiled=True)  112 us
    psum x1, waiting for transfers between devices, body(): lax.psum(jnp.dot(atm_out, w_flux_in, preferred_element_type=jnp.float32),...  80.6 us
    all_gather x1, waiting for transfers between devices, body(): whole = lax.all_gather(tokens, 'tile', axis=1, tiled=True)  39.7 us
    ppermute x5, waiting for transfers between devices, with_halo(): lax.ppermute(lax.slice_in_dim(block, 0, width, axis=dim), axis, backward)  21.5 us
    reduce_sum x3, other arithmetic, layer_norm(): center = values - jnp.mean(values, axis=-1, keepdims=True)  20.7 us
    ppermute x5, starting transfers between devices, with_halo(): lax.ppermute(lax.slice_in_dim(block, block.shape[dim] - width, None, axis...  18.8 us
  transfers between devices with their start and end apart: 15, of which 10 were waited for; matrix products, arithmetic and copies ran while one was open for 0% of the time, Pallas kernels for 0%

commit v1 on v0

--- a/solution.py
+++ b/solution.py
@@ -1,7 +1,357 @@
+import functools
+
 import jax
 import jax.numpy as jnp
 from jax import lax
+from jax.experimental import pallas as pl
+from jax.experimental.pallas import tpu as pltpu
 from jax.sharding import PartitionSpec as P
+
+MESH = pl.DeviceIdType.MESH
+BF = jnp.bfloat16
+F32 = jnp.float32
+EPS = 1e-06
+XS = 4
+ZS = 8
+
+
+def nt_dot(lhs, rhs):
+    return lax.dot_general(lhs, rhs, (((1,), (1,)), ((), ())), preferred_element_type=F32)
+
+
+def atmosphere_kernel(
+    xs, zs,
+    tok_ref, gain_ref, up_ref, down_ref, wfi_ref, wfo_ref,
+    atm_ref, win_ref,
+    yb, gw, tk, nm, hd, fi, sb, rb, acc, at, ao, wn,
+    y_send, y_recv, ring_send, ring_recv, tok_send, tok_recv, fi_send, fi_recv,
+    rs_send, rs_recv, at_send, at_recv, fx_send, fx_recv, rim_send, rim_recv,
+):
+    f = lax.axis_index("fsdp")
+    t = lax.axis_index("tile")
+    n_f = 2 * xs * zs
+    x, z, yl = f // (2 * zs), (f // 2) % zs, f % 2
+    yh, c = t // 2, t % 2
+    yp = f + 1 - 2 * yl
+    x_right = (f + 2 * zs) % n_f
+    x_left = (f - 2 * zs + n_f) % n_f
+    z_right = x * 2 * zs + ((z + 1) % zs) * 2 + yl
+    z_left = x * 2 * zs + ((z + zs - 1) % zs) * 2 + yl
+    f_next, f_prev = (f + 1) % n_f, (f + n_f - 1) % n_f
+    t_core = yh * 2 + (1 - c)
+    t_far = (1 - yh) * 2 + c
+    t_diag = (1 - yh) * 2 + (1 - c)
+    rows = tok_ref.shape[0]
+    quarter = rows // 4
+    feat = tok_ref.shape[1]
+    width = gw.shape[-1]
+    d_model = 4 * feat
+
+    barrier = pltpu.get_barrier_semaphore()
+    for other in (yp, x_right, x_left, z_right, z_left):
+        pl.semaphore_signal(barrier, inc=1, device_id=(other, t), device_id_type=MESH)
+    for other in (t_core, t_far, t_diag):
+        pl.semaphore_signal(barrier, inc=1, device_id=(f, other), device_id_type=MESH)
+    pl.semaphore_signal(barrier, inc=1, device_id=(f_prev, 3), device_id_type=MESH)
+    pl.semaphore_signal(barrier, inc=1, device_id=(f_next, 0), device_id_type=MESH)
+    edge = jnp.where(jnp.logical_or(t == 0, t == 3), 4, 0)
+    pl.semaphore_wait(barrier, 8 + edge)
+
+    def remote(src, dst, send, recv, device):
+        return pltpu.make_async_remote_copy(
+            src_ref=src, dst_ref=dst, send_sem=send, recv_sem=recv,
+            device_id=device, device_id_type=MESH,
+        )
+
+    y_copies = [
+        remote(ref, yb.at[w], y_send.at[w], y_recv.at[w], (yp, t))
+        for w, ref in enumerate((up_ref, down_ref))
+    ]
+    for copy in y_copies:
+        copy.start()
+    shared = []
+    for src, dst, send, recv in ((tok_ref, tk, tok_send, tok_recv), (wfi_ref, fi, fi_send, fi_recv)):
+        far = remote(src, dst.at[t], send.at[1], recv.at[1], (f, t_far))
+        near = remote(src, dst.at[t], send.at[0], recv.at[0], (f, t_core))
+        relay = remote(dst.at[t_far], dst.at[t_far], send.at[2], recv.at[2], (f, t_core))
+        shared.append((near, far, relay))
+    for near, far, relay in shared:
+        far.start()
+        near.start()
+
+    def ring_round(w, stream, stage, s):
+        on_x = (stream == 0) == (stage == 0)
+        n = xs if on_x else zs
+        here = x if on_x else z
+        last = s == n // 2 - 1
+        copies = []
+        for way in (0, 1):
+            chunk = (here - s + n) % n if way == 0 else (here + s) % n
+            if last:
+                pieces = 2 * stream + way
+            else:
+                pieces = pl.ds(2 * stream, 2)
+            if stage == 0:
+                part = gw.at[w, pieces, chunk, z] if on_x else gw.at[w, pieces, x, chunk]
+            else:
+                part = gw.at[w, pieces, chunk] if on_x else gw.at[w, pieces, :, chunk]
+            if on_x:
+                target = x_right if way == 0 else x_left
+            else:
+                target = z_right if way == 0 else z_left
+            at_sem = (((w * 2 + stream) * 2 + stage) * 4 + s) * 2 + way
+            copies.append(
+                remote(part, part, ring_send.at[at_sem], ring_recv.at[at_sem], (target, t))
+            )
+        return copies
+
+    done = []
+
+    def start(copies):
+        for copy in copies:
+            copy.start()
+        done.extend(copies)
+        return copies
+
+    def arrive(copies):
+        for copy in copies:
+            copy.wait_recv()
+
+    for w, ref in enumerate((up_ref, down_ref)):
+        y_copies[w].wait_recv()
+        for p in range(4):
+            mine = ref[:, p * width : (p + 1) * width].astype(F32)
+            other = yb[w, :, p * width : (p + 1) * width].astype(F32)
+            first = jnp.where(yl == 0, mine, other)
+            second = jnp.where(yl == 0, other, mine)
+            gw[w, p, x, z] = jnp.concatenate([first, second], axis=0).astype(BF)
+        if w == 0:
+            up_small = [start(ring_round(0, b, 0, 0)) for b in (0, 1)]
+    down_small = [start(ring_round(1, b, 0, 0)) for b in (0, 1)]
+    tk[t] = tok_ref[...]
+    fi[t] = wfi_ref[...]
+
+    sizes = (xs // 2, zs // 2)
+    for s in range(1, max(sizes)):
+        for w, small in ((0, up_small), (1, down_small)):
+            for b in (0, 1):
+                if s < sizes[b]:
+                    arrive(small[b])
+                    small[b] = start(ring_round(w, b, 0, s))
+    arrive(up_small[0])
+    up_a = start(ring_round(0, 0, 1, 0))
+    arrive(up_small[1])
+    up_b = start(ring_round(0, 1, 1, 0))
+    arrive(down_small[0])
+    down_a = start(ring_round(1, 0, 1, 0))
+    arrive(down_small[1])
+    down_b = start(ring_round(1, 1, 1, 0))
+
+    for near, far, relay in shared:
+        far.wait_recv()
+        relay.start()
+
+    arrive(up_a)
+    up_a = start(ring_round(0, 0, 1, 1)) if zs // 2 > 1 else []
+    arrive(up_b)
+    up_b = start(ring_round(0, 1, 1, 1)) if xs // 2 > 1 else []
+    arrive(down_a)
+    down_a = start(ring_round(1, 0, 1, 1)) if zs // 2 > 1 else []
+
+    shared[0][0].wait_recv()
+    shared[0][2].wait_recv()
+    step = min(32, quarter)
+
+    @pl.loop(0, rows // step)
+    def _(i):
+        span = pl.ds(pl.multiple_of(i * step, step), step)
+        values = [tk[q, span, :].astype(F32) for q in range(4)]
+        mean = sum(jnp.sum(v, axis=-1, keepdims=True) for v in values) / d_model
+        centers = [v - mean for v in values]
+        spread = sum(jnp.sum(v * v, axis=-1, keepdims=True) for v in centers) / d_model
+        inverse = lax.rsqrt(spread + EPS)
+        for q in range(4):
+            gain = gain_ref[:, q * feat : (q + 1) * feat]
+            nm[span, q * feat : (q + 1) * feat] = (centers[q] * inverse * gain).astype(BF)
+
+    for s in range(2, zs // 2):
+        arrive(up_a)
+        up_a = start(ring_round(0, 0, 1, s))
+        if s == 2:
+            arrive(down_b)
+            down_b = start(ring_round(1, 1, 1, 1)) if xs // 2 > 1 else []
+        arrive(down_a)
+        down_a = start(ring_round(1, 0, 1, s))
+    if zs // 2 <= 2 and xs // 2 > 1:
+        arrive(down_b)
+        down_b = start(ring_round(1, 1, 1, 1))
+    arrive(up_b)
+    arrive(up_a)
+
+    @pl.loop(0, 8)
+    def _(i):
+        half, block = i // 4, i % 4
+        span = pl.ds(pl.multiple_of(block * quarter, quarter), quarter)
+        rhs = jnp.concatenate(
+            [gw[0, half * 2 + k].reshape(d_model, width) for k in (0, 1)], axis=1
+        )
+        pre = jnp.dot(nm[span, :], rhs, preferred_element_type=F32)
+        hd[half, span, :] = jax.nn.gelu(pre, approximate=True).astype(BF)
+
+    arrive(down_b)
+    arrive(down_a)
+
+    def partial(block, half):
+        span = pl.ds(pl.multiple_of(block * quarter, quarter), quarter)
+        lhs = jnp.concatenate([hd[0, span, :], hd[1, span, :]], axis=1)
+        part = pl.ds(half * (xs // 2), xs // 2)
+        rhs = jnp.concatenate(
+            [gw[1, p, part].reshape(d_model // 2, width) for p in range(4)], axis=1
+        )
+        return nt_dot(lhs, rhs)
+
+    def sums(k, half, target):
+        return remote(
+            sb.at[k, half], rb.at[k, half], rs_send.at[2 * k + half], rs_recv.at[2 * k + half],
+            (f, target),
+        )
+
+    to_core = [sums(0, half, t_core) for half in (0, 1)]
+    to_far = [sums(1, half, t_far) for half in (0, 1)]
+    to_core2 = [sums(2, half, t_core) for half in (0, 1)]
+
+    for half in (0, 1):
+        sb[0, half] = partial(t_diag, half).astype(BF)
+        to_core[half].start()
+    for half in (0, 1):
+        acc[half] = partial(t_far, half)
+        to_core[half].wait_recv()
+        sb[1, half] = (acc[half] + rb[0, half].astype(F32)).astype(BF)
+        to_far[half].start()
+    for half in (0, 1):
+        sb[2, half] = partial(t_core, half).astype(BF)
+        to_core2[half].start()
+    for half in (0, 1):
+        acc[half] = partial(t, half)
+    mine = pl.ds(pl.multiple_of(t * quarter, quarter), quarter)
+    for half in (0, 1):
+        to_core2[half].wait_recv()
+        to_far[half].wait_recv()
+        for k in (0, 1):
+            q = 2 * half + k
+            cols = slice(k * feat, (k + 1) * feat)
+            delta = acc[half, :, cols] + rb[2, half, :, cols].astype(F32) + rb[1, half, :, cols].astype(F32)
+            at[q] = (tk[q, mine, :].astype(F32) + delta).astype(BF)
+
+    at_copies = []
+    for k in range(1, 4):
+        q = (t + k) % 4
+        at_copies.append(remote(at.at[q], ao.at[t], at_send.at[k - 1], at_recv.at[k - 1], (f, q)))
+        at_copies[-1].start()
+    ao[t] = at[t]
+
+    shared[1][0].wait_recv()
+    shared[1][2].wait_recv()
+    pre = jnp.dot(
+        jnp.concatenate([at[q] for q in range(4)], axis=1),
+        fi[...].reshape(d_model, fi.shape[-1]),
+        preferred_element_type=F32,
+    )
+    flux_hidden = jax.nn.gelu(pre, approximate=True).astype(BF)
+    wn[1 + t] = jnp.dot(flux_hidden, wfo_ref[...], preferred_element_type=F32).astype(BF)
+    fx_copies = []
+    for k in range(1, 4):
+        fx_copies.append(
+            remote(wn.at[1 + t], wn.at[1 + t], fx_send.at[k - 1], fx_recv.at[k - 1], (f, (t + k) % 4))
+        )
+        fx_copies[-1].start()
+
+    def rim(slot, source, target):
+        return [
+            remote(wn.at[source], wn.at[slot], rim_send.at[q], rim_recv.at[slot // 5], (target, q))
+            for q in range(4)
+        ]
+
+    low = rim(0, 4, f_next)
+    high = rim(5, 1, f_prev)
+
+    @pl.when(t == 3)
+    def _():
+        for copy in low:
+            copy.start()
+
+    @pl.when(t == 0)
+    def _():
+        for copy in high:
+            copy.start()
+
+    for copy in at_copies:
+        copy.wait_recv()
+    for q in range(4):
+        atm_ref[pl.ds(q * quarter, quarter), :] = ao[q]
+    for copy in fx_copies:
+        copy.wait_recv()
+    low[0].wait_recv()
+    high[0].wait_recv()
+    win_ref[...] = wn[...]
+
+    @pl.when(t == 3)
+    def _():
+        for copy in low:
+            copy.wait_send()
+
+    @pl.when(t == 0)
+    def _():
+        for copy in high:
+            copy.wait_send()
+
+    for copy in y_copies + done + at_copies + fx_copies + to_core + to_far + to_core2:
+        copy.wait_send()
+    for trio in shared:
+        for copy in trio:
+            copy.wait_send()
+
+
+def atmosphere(xs, zs, tokens, ln_gain, w_up, w_down, w_flux_in, w_flux_out):
+    rows, feat = tokens.shape
+    d_model = 4 * feat
+    shard, hidden = w_up.shape
+    width = hidden // 4
+    fh, flx = w_flux_out.shape
+    quarter = rows // 4
+    dma = pltpu.SemaphoreType.DMA
+    vm = pl.BlockSpec(memory_space=pltpu.VMEM)
+    return pl.pallas_call(
+        functools.partial(atmosphere_kernel, xs, zs),
+        out_shape=(
+            jax.ShapeDtypeStruct((rows, feat), BF),
+            jax.ShapeDtypeStruct((6, quarter, flx), BF),
+        ),
+        in_specs=[vm] * 6,
+        out_specs=(vm, vm),
+        scratch_shapes=[
+            pltpu.VMEM((2, shard, hidden), BF),
+            pltpu.VMEM((2, 4, xs, zs, 2 * shard, width), BF),
+            pltpu.VMEM((4, rows, feat), BF),
+            pltpu.VMEM((rows, d_model), BF),
+            pltpu.VMEM((2, rows, hidden // 2), BF),
+            pltpu.VMEM((4, feat, fh), BF),
+            pltpu.VMEM((3, 2, quarter, d_model // 2), BF),
+            pltpu.VMEM((3, 2, quarter, d_model // 2), BF),
+            pltpu.VMEM((2, quarter, d_model // 2), F32),
+            pltpu.VMEM((4, quarter, feat), BF),
+            pltpu.VMEM((4, quarter, feat), BF),
+            pltpu.VMEM((6, quarter, flx), BF),
+            dma((2,)), dma((2,)), dma((64,)), dma((64,)),
+            dma((3,)), dma((3,)), dma((3,)), dma((3,)),
+            dma((6,)), dma((6,)), dma((3,)), dma((3,)),
+            dma((3,)), dma((3,)), dma((4,)), dma((2,)),
+        ],
+        compiler_params=pltpu.CompilerParams(
+            collective_id=0, has_side_effects=True, vmem_limit_bytes=58 * 1024 * 1024
+        ),
+        name="atmosphere",
+    )(tokens, ln_gain.reshape(1, d_model), w_up, w_down.T, w_flux_in, w_flux_out)
 
 
 def with_halo(block, sides, width):
@@ -20,7 +370,7 @@
 def layer_norm(values, gain):
     center = values - jnp.mean(values, axis=-1, keepdims=True)
     spread = jnp.mean(center * center, axis=-1, keepdims=True)
-    return center * lax.rsqrt(spread + 1e-06) * gain
+    return center * lax.rsqrt(spread + EPS) * gain
 
 
 def conv_block(padded, region_mask, kernel, gain, w_one, w_two):
@@ -61,22 +411,9 @@
     w_pw2,
 ):
     band_rows = tokens.shape[0]
-    whole = lax.all_gather(tokens, "tile", axis=1, tiled=True)
-    normed = layer_norm(whole.astype(jnp.float32), ln_gain).astype(jnp.bfloat16)
-    up_whole = lax.all_gather(w_up, "fsdp", axis=0, tiled=True)
-    pre = jnp.dot(normed, up_whole, preferred_element_type=jnp.float32)
-    hidden = jax.nn.gelu(pre, approximate=True).astype(jnp.bfloat16)
-    down_whole = lax.all_gather(w_down, "fsdp", axis=1, tiled=True)
-    terms = jnp.dot(hidden, down_whole, preferred_element_type=jnp.float32)
-    delta = lax.psum_scatter(terms, "tile", scatter_dimension=1, tiled=True)
-    atm_out = (tokens.astype(jnp.float32) + delta).astype(jnp.bfloat16)
-    flux_pre = lax.psum(jnp.dot(atm_out, w_flux_in, preferred_element_type=jnp.float32), "tile")
-    flux_hidden = jax.nn.gelu(flux_pre, approximate=True).astype(jnp.bfloat16)
-    fluxes = jnp.dot(flux_hidden, w_flux_out, preferred_element_type=jnp.float32).astype(
-        jnp.bfloat16
-    )
     rim_rows = band_rows // 4
-    window = with_halo(fluxes, (("fsdp", 0),), rim_rows)
+    atm_out, window = atmosphere(XS, ZS, tokens, ln_gain, w_up, w_down, w_flux_in, w_flux_out)
+    window = window.reshape(6 * rim_rows, window.shape[-1])
     band = lax.axis_index("fsdp")
     local_index = (column_map - (band * band_rows - rim_rows)).reshape(-1)
     picked = jnp.take(window, local_index, axis=0)

time: 922 us -> 201 us (0.22)
  the two profiles are of different devices: /device:TPU:1 before, /device:TPU:3 now
where the time goes in v1:
time: 201 us
  Pallas kernels  123 us (61%)
  starting transfers between devices  28.7 us (14%)
  other arithmetic  22.6 us (11%)
  waiting for transfers between devices  12.5 us (6%)
  local copies, waits for them, and re-layouts  7.03 us (3%)
  matrix products  5.59 us (3%)
    pallas_call x1, Pallas kernels, atmosphere(): pl.pallas_call(functools.partial(atmosphere_kernel, xs, zs), out_shape=(j...  123 us
    reduce_sum x2, other arithmetic, layer_norm(): center = values - jnp.mean(values, axis=-1, keepdims=True)  18.2 us
    ppermute x4, starting transfers between devices, with_halo(): lax.ppermute(lax.slice_in_dim(block, 0, width, axis=dim), axis, backward)  16.8 us
    ppermute x4, waiting for transfers between devices, with_halo(): lax.ppermute(lax.slice_in_dim(block, 0, width, axis=dim), axis, backward)  12.5 us
    ppermute x4, starting transfers between devices, with_halo(): lax.ppermute(lax.slice_in_dim(block, block.shape[dim] - width, None, axis...  12 us
  transfers between devices with their start and end apart: 8, of which 5 were waited for; matrix products, arithmetic and copies ran while one was open for 0% of the time, Pallas kernels for 0%

profile of v1, /device:TPU:3, one launch (start us, length us, event | category | flops | bytes accessed | tf_op | source)
XLA Modules:
  0.0 200.9 jit_solution(11794457698057552616)
XLA Ops:
  0.6 0.0 copy-start
  0.7 0.8 broadcast_subtract_fusion
  1.4 0.1 reshape.92
  1.5 0.1 reshape.90
  1.6 1.3 reshape.89.gain_ref
  2.9 0.7 convert_element_type.323
  3.6 123.4 %atmosphere.1 = (bf16[1024,384]{1,0:T(8,128)(2,1)}, bf16[6,256,128]{2,1,0:T(8,128)(2,1)}) custom-call(bf16[1024,384]{1,0:T(8,128)(2,1)} %tok_ref.1, f32[1,1536]{1,0:T(1,128)} %reshape.89.gain_ref, bf16[24,1536]{1,0:T(8,128)(2,1)} %up_ref.1, bf16[24,1536]{1,0:T(8,128)(2,1)} %bitcast.135, bf16[384,768]{1,0:T(8,128)(2,1)} %wfi_ref.1, bf16[768,128]{1,0:T(8,128)(2,1)} %wfo_ref.1), custom_call_target="tpu_custom_call" | custom-call | tf_op jit(solution)/shard_map/atmosphere/pallas_call | solution.py:324
  127.0 0.0 copy-start.2
  127.0 4.0 %gather_fusion = bf16[1024,128]{1,0:T(8,128)(2,1)S(1)} fusion(bf16[1536,128]{1,0:T(8,128)(2,1)} %bitcast.131, s32[1024]{0:T(1024)S(1)} %broadcast_clamp_fusion), kind=kCustom, calls=%fused_computation | custom fusion | bytes 528384 | tf_op jit(solution)/shard_map/jit(_take)/gather | solution.py:419
  131.0 0.0 copy-done
  131.0 0.0 copy-start.3
  131.0 0.4 fusion.86
  131.4 0.0 copy-start.4
  131.4 0.0 copy-done.2
  131.4 0.3 multiply_convert_fusion.2
  131.7 1.9 collective-permute-start
  133.6 6.4 %collective-permute-start.1 = (bf16[3,32,256]{2,1,0:T(8,128)(2,1)S(1)}, bf16[3,32,256]{2,1,0:T(8,128)(2,1)S(1)}, u32[]{:S(2)}, u32[]{:S(2)}) collective-permute-start(bf16[3,32,256]{2,1,0:T(8,128)(2,1)S(1)} %get-tuple-element.21), channel_id=1, source_target_pairs={{4,0},{8,4},{12,8},{16,12},{20,16},{24,20},{28,24},{32,28},{36,32}... | collective-permute-start | bytes 147464 | tf_op jit(solution)/shard_map/ppermute | solution.py:365
  140.0 0.0 copy-done.3
  140.0 0.1 fusion.97
  140.2 0.1 collective-permute-done
  140.3 1.0 collective-permute-done.1
  141.3 0.1 pad_maximum_fusion.11
  141.4 4.8 %collective-permute-start.2 = (bf16[38,3,256]{2,1,0:T(4,128)(2,1)S(1)}, bf16[38,3,256]{2,1,0:T(4,128)(2,1)S(1)}, u32[]{:S(2)}, u32[]{:S(2)}) collective-permute-start(bf16[38,3,256]{2,1,0:T(4,128)(2,1)S(1)} %get-tuple-element.16), channel_id=1, source_target_pairs={{0,1},{1,2},{2,3},{4,5},{5,6},{6,7},{8,9},{9,10},{10,11},{12,13},{... | collective-permute-start | bytes 175112 | tf_op jit(solution)/shard_map/ppermute | solution.py:362
  146.2 2.1 %collective-permute-start.3 = (bf16[38,3,256]{2,1,0:T(4,128)(2,1)S(1)}, bf16[38,3,256]{2,1,0:T(4,128)(2,1)S(1)}, u32[]{:S(2)}, u32[]{:S(2)}) collective-permute-start(bf16[38,3,256]{2,1,0:T(4,128)(2,1)S(1)} %get-tuple-element.17), channel_id=1, source_target_pairs={{1,0},{2,1},{3,2},{5,4},{6,5},{7,6},{9,8},{10,9},{11,10},{13,12},{... | collective-permute-start | bytes 175112 | tf_op jit(solution)/shard_map/ppermute | solution.py:365
  148.3 0.0 copy-done.4
  148.3 0.0 collective-permute-done.2
  148.3 5.1 %collective-permute-done.3 = bf16[38,3,256]{2,1,0:T(4,128)(2,1)S(1)} collective-permute-done((bf16[38,3,256]{2,1,0:T(4,128)(2,1)S(1)}, bf16[38,3,256]{2,1,0:T(4,128)(2,1)S(1)}, u32[]{:S(2)}, u32[]{:S(2)}) %collective-permute-start.3) | collective-permute-done | bytes 58400 | tf_op jit(solution)/shard_map/ppermute | solution.py:365
  153.4 0.5 maximum_maximum_fusion
  153.9 9.1 %fusion.93 = (f32[32,32]{1,0:T(8,128)S(1)}, f32[32,32,256]{2,1,0:T(8,128)S(1)}) fusion(f32[256]{0:T(256)S(1)} %bitcast.176, bf16[38,35,256]{2,1,0:T(8,128)(2,1)S(1)} %get-tuple-element.15, f32[256]{0:T(256)S(1)} %bitcast.177, f32[256]{0:T(256)S(1)} %bitcast.178, f32[256]{0:T(256)S(1)} %bitcast.179, bf16[3,32,256]{2,1,0:T(8,128)(2,1)S(1)} %collective-permute-done.1, ...), kind=kLoop, calls=%fused_computation.145 | loop fusion | flops 40107008 | bytes 23745536 | tf_op jit(solution)/shard_map/reduce_sum | solution.py:371
  163.0 0.0 copy-start.5
  163.0 0.4 multiply_reduce_fusion.1
  163.4 0.3 multiply_convert_fusion.1
  163.8 0.5 copy-done.5
  164.3 0.0 copy-start.6
  164.3 1.5 fusion.7
  165.8 0.0 copy-done.6
  165.8 0.7 fusion.18
  166.5 1.9 collective-permute-start.4
  168.5 6.4 %collective-permute-start.5 = (bf16[3,32,256]{2,1,0:T(8,128)(2,1)S(1)}, bf16[3,32,256]{2,1,0:T(8,128)(2,1)S(1)}, u32[]{:S(2)}, u32[]{:S(2)}) collective-permute-start(bf16[3,32,256]{2,1,0:T(8,128)(2,1)S(1)} %get-tuple-element.19), channel_id=1, source_target_pairs={{4,0},{8,4},{12,8},{16,12},{20,16},{24,20},{28,24},{32,28},{36,32}... | collective-permute-start | bytes 147464 | tf_op jit(solution)/shard_map/ppermute | solution.py:365
  174.9 0.0 collective-permute-done.4
  174.9 1.1 collective-permute-done.5
  176.0 0.1 pad_maximum_fusion.8
  176.1 3.3 %collective-permute-start.6 = (bf16[38,3,256]{2,1,0:T(4,128)(2,1)S(1)}, bf16[38,3,256]{2,1,0:T(4,128)(2,1)S(1)}, u32[]{:S(2)}, u32[]{:S(2)}) collective-permute-start(bf16[38,3,256]{2,1,0:T(4,128)(2,1)S(1)} %get-tuple-element.12), channel_id=1, source_target_pairs={{0,1},{1,2},{2,3},{4,5},{5,6},{6,7},{8,9},{9,10},{10,11},{12,13},{... | collective-permute-start | bytes 175112 | tf_op jit(solution)/shard_map/ppermute | solution.py:362
  179.4 1.9 collective-permute-start.7
  181.3 0.0 collective-permute-done.6
  181.3 5.3 %collective-permute-done.7 = bf16[38,3,256]{2,1,0:T(4,128)(2,1)S(1)} collective-permute-done((bf16[38,3,256]{2,1,0:T(4,128)(2,1)S(1)}, bf16[38,3,256]{2,1,0:T(4,128)(2,1)S(1)}, u32[]{:S(2)}, u32[]{:S(2)}) %collective-permute-start.7) | collective-permute-done | bytes 58400 | tf_op jit(solution)/shard_map/ppermute | solution.py:365
  186.6 0.5 maximum_maximum_fusion.1
  187.1 9.1 %fusion.91 = (f32[32,32]{1,0:T(8,128)S(1)}, f32[32,32,256]{2,1,0:T(8,128)S(1)}) fusion(f32[256]{0:T(256)S(1)} %bitcast.206, bf16[38,35,256]{2,1,0:T(8,128)(2,1)S(1)} %get-tuple-element.11, f32[256]{0:T(256)S(1)} %bitcast.207, f32[256]{0:T(256)S(1)} %bitcast.208, f32[256]{0:T(256)S(1)} %bitcast.209, bf16[3,32,256]{2,1,0:T(8,128)(2,1)S(1)} %collective-permute-done.5, ...), kind=kLoop, calls=%fused_computation.144 | loop fusion | flops 40107008 | bytes 23745536 | tf_op jit(solution)/shard_map/reduce_sum | solution.py:371
  196.2 0.4 multiply_reduce_fusion
  196.6 0.3 multiply_convert_fusion
  197.0 1.5 fusion.15
  198.5 0.0 copy-start.1
  198.5 1.5 fusion.19
  200.0 0.0 copy-done.1
  200.0 0.9 copy.23
  (17 shorter events, 0.2 us)
Async XLA Ops:
  0.6 130.4 %copy-start = (bf16[128,256]{1,0:T(8,128)(2,1)S(1)}, bf16[128,256]{1,0:T(8,128)(2,1)}, u32[]{:S(2)}) copy-start(bf16[128,256]{1,0:T(8,128)(2,1)} %param.23) | copy-start | bytes 196612
  127.0 4.4 %copy-start.2 = (bf16[32,32,256]{2,1,0:T(8,128)(2,1)S(1)}, bf16[32,32,256]{2,1,0:T(8,128)(2,1)}, u32[]{:S(2)}) copy-start(bf16[32,32,256]{2,1,0:T(8,128)(2,1)} %param.20) | copy-start | bytes 1572868
  131.0 9.0 %copy-start.3 = (f32[2,7,7,256]{3,0,2,1:T(2,128)S(1)}, f32[2,7,7,256]{3,0,2,1:T(2,128)}, u32[]{:S(2)}) copy-start(f32[2,7,7,256]{3,0,2,1:T(2,128)} %param.24) | copy-start | bytes 301060
  131.4 16.9 %copy-start.4 = (f32[2,256]{1,0:T(2,128)S(1)}, f32[2,256]{1,0:T(2,128)}, u32[]{:S(2)}) copy-start(f32[2,256]{1,0:T(2,128)} %param.25) | copy-start | bytes 6148
  131.7 8.6 %collective-permute-start = (bf16[3,32,256]{2,1,0:T(8,128)(2,1)S(1)}, bf16[3,32,256]{2,1,0:T(8,128)(2,1)S(1)}, u32[]{:S(2)}, u32[]{:S(2)}) collective-permute-start(bf16[3,32,256]{2,1,0:T(8,128)(2,1)S(1)} %get-tuple-element.20), channel_id=1, source_target_pairs={{0,4},{4,8},{8,12},{12,16},{16,20},{20,24},{24,28},{28,32},{32,36}... | collective-permute-start | bytes 147464 | tf_op jit(solution)/shard_map/ppermute | solution.py:362
  133.6 7.7 %collective-permute-start.1 = (bf16[3,32,256]{2,1,0:T(8,128)(2,1)S(1)}, bf16[3,32,256]{2,1,0:T(8,128)(2,1)S(1)}, u32[]{:S(2)}, u32[]{:S(2)}) collective-permute-start(bf16[3,32,256]{2,1,0:T(8,128)(2,1)S(1)} %get-tuple-element.21), channel_id=1, source_target_pairs={{4,0},{8,4},{12,8},{16,12},{20,16},{24,20},{28,24},{32,28},{36,32}... | collective-permute-start | bytes 147464 | tf_op jit(solution)/shard_map/ppermute | solution.py:365
  141.4 7.0 %collective-permute-start.2 = (bf16[38,3,256]{2,1,0:T(4,128)(2,1)S(1)}, bf16[38,3,256]{2,1,0:T(4,128)(2,1)S(1)}, u32[]{:S(2)}, u32[]{:S(2)}) collective-permute-start(bf16[38,3,256]{2,1,0:T(4,128)(2,1)S(1)} %get-tuple-element.16), channel_id=1, source_target_pairs={{0,1},{1,2},{2,3},{4,5},{5,6},{6,7},{8,9},{9,10},{10,11},{12,13},{... | collective-permute-start | bytes 175112 | tf_op jit(solution)/shard_map/ppermute | solution.py:362
  146.2 7.2 %collective-permute-start.3 = (bf16[38,3,256]{2,1,0:T(4,128)(2,1)S(1)}, bf16[38,3,256]{2,1,0:T(4,128)(2,1)S(1)}, u32[]{:S(2)}, u32[]{:S(2)}) collective-permute-start(bf16[38,3,256]{2,1,0:T(4,128)(2,1)S(1)} %get-tuple-element.17), channel_id=1, source_target_pairs={{1,0},{2,1},{3,2},{5,4},{6,5},{7,6},{9,8},{10,9},{11,10},{13,12},{... | collective-permute-start | bytes 175112 | tf_op jit(solution)/shard_map/ppermute | solution.py:365
  163.0 1.2 copy-start.5
  164.3 1.5 copy-start.6
  166.5 8.3 %collective-permute-start.4 = (bf16[3,32,256]{2,1,0:T(8,128)(2,1)S(1)}, bf16[3,32,256]{2,1,0:T(8,128)(2,1)S(1)}, u32[]{:S(2)}, u32[]{:S(2)}) collective-permute-start(bf16[3,32,256]{2,1,0:T(8,128)(2,1)S(1)} %get-tuple-element.18), channel_id=1, source_target_pairs={{0,4},{4,8},{8,12},{12,16},{16,20},{20,24},{24,28},{28,32},{32,36}... | collective-permute-start | bytes 147464 | tf_op jit(solution)/shard_map/ppermute | solution.py:362
  168.5 7.5 %collective-permute-start.5 = (bf16[3,32,256]{2,1,0:T(8,128)(2,1)S(1)}, bf16[3,32,256]{2,1,0:T(8,128)(2,1)S(1)}, u32[]{:S(2)}, u32[]{:S(2)}) collective-permute-start(bf16[3,32,256]{2,1,0:T(8,128)(2,1)S(1)} %get-tuple-element.19), channel_id=1, source_target_pairs={{4,0},{8,4},{12,8},{16,12},{20,16},{24,20},{28,24},{32,28},{36,32}... | collective-permute-start | bytes 147464 | tf_op jit(solution)/shard_map/ppermute | solution.py:365
  176.1 5.3 %collective-permute-start.6 = (bf16[38,3,256]{2,1,0:T(4,128)(2,1)S(1)}, bf16[38,3,256]{2,1,0:T(4,128)(2,1)S(1)}, u32[]{:S(2)}, u32[]{:S(2)}) collective-permute-start(bf16[38,3,256]{2,1,0:T(4,128)(2,1)S(1)} %get-tuple-element.12), channel_id=1, source_target_pairs={{0,1},{1,2},{2,3},{4,5},{5,6},{6,7},{8,9},{9,10},{10,11},{12,13},{... | collective-permute-start | bytes 175112 | tf_op jit(solution)/shard_map/ppermute | solution.py:362
  179.4 7.2 %collective-permute-start.7 = (bf16[38,3,256]{2,1,0:T(4,128)(2,1)S(1)}, bf16[38,3,256]{2,1,0:T(4,128)(2,1)S(1)}, u32[]{:S(2)}, u32[]{:S(2)}) collective-permute-start(bf16[38,3,256]{2,1,0:T(4,128)(2,1)S(1)} %get-tuple-element.13), channel_id=1, source_target_pairs={{1,0},{2,1},{3,2},{5,4},{6,5},{7,6},{9,8},{10,9},{11,10},{13,12},{... | collective-permute-start | bytes 175112 | tf_op jit(solution)/shard_map/ppermute | solution.py:365
  198.5 1.5 copy-start.1

commit v2 on v1

--- a/solution.py
+++ b/solution.py
@@ -6,6 +6,7 @@
 from jax.experimental import pallas as pl
 from jax.experimental.pallas import tpu as pltpu
 from jax.sharding import PartitionSpec as P
+import numpy as np
 
 MESH = pl.DeviceIdType.MESH
 BF = jnp.bfloat16
@@ -19,13 +20,193 @@
     return lax.dot_general(lhs, rhs, (((1,), (1,)), ((), ())), preferred_element_type=F32)
 
 
+def ocean_prepare(first, mask_ref, map_ref, taps_ref, mk, oh, wb):
+    grid_rows, grid_cols = map_ref.shape
+    tiles = oh.shape[1] // 128
+
+    @pl.loop(0, grid_rows)
+    def _(r):
+        square = (grid_cols, grid_cols)
+        eye = (
+            lax.broadcasted_iota(jnp.int32, square, 0) == lax.broadcasted_iota(jnp.int32, square, 1)
+        ).astype(F32)
+        ones = jnp.ones((grid_cols, 128), BF)
+
+        def upright(line):
+            return jnp.dot((eye * line).astype(BF), ones, preferred_element_type=F32)
+
+        index = map_ref[pl.ds(r, 1), :] - first
+        high = upright((index >> 5).astype(F32))
+        low = upright((index & 31).astype(F32))
+        index_up = high * 32.0 + low
+        span = pl.ds(pl.multiple_of(r * grid_cols, grid_cols), grid_cols)
+        mk[span, :] = upright(mask_ref[pl.ds(r, 1), :].astype(F32))
+        lane = lax.broadcasted_iota(jnp.int32, (grid_cols, 128), 1).astype(F32)
+        for k in range(tiles):
+            oh[span, k * 128 : (k + 1) * 128] = jnp.where(
+                index_up == lane + 128.0 * k, 1.0, 0.0
+            ).astype(BF)
+
+    for k in range(taps_ref.shape[0]):
+        for a in range(7):
+            for b in range(7):
+                wb[k, a, b] = jnp.broadcast_to(taps_ref[k, a, b : b + 1, :], wb.shape[3:])
+
+
+def ocean(
+    f, t, n_f, f_prev, f_next, remote, wn, sea_ref, couple_ref, sgain_ref, one_ref, two_ref,
+    pick_ref, place_ref, out_ref, mk, oh, wb, st, pd, sh, cv, pk, rw, rn, halo_send, halo_recv,
+):
+    grid_rows, grid_cols, chans = sea_ref.shape
+    cells = 8 * grid_cols
+    wide = pd.shape[1]
+    t_next, t_prev = (t + 1) % 4, (t + 3) % 4
+    edge = 3 * grid_cols
+
+    def masked(span, values):
+        return (jnp.concatenate([mk[span, :]] * (chans // 128), axis=1) * values).astype(BF)
+
+    def keep(k, i, span, values):
+        st[k, span, :] = values
+        pd[pl.ds(3 + i * 8, 8), 8 : 8 + grid_cols, :] = values.astype(F32).reshape(
+            8, grid_cols, chans
+        )
+
+    @pl.loop(0, grid_rows // 8)
+    def _(i):
+        span = pl.ds(pl.multiple_of(i * cells, cells), cells)
+        picked = jnp.dot(
+            oh[span, :], wn[...].reshape(oh.shape[1], wn.shape[2]), preferred_element_type=F32
+        ).astype(BF)
+        forcing = jnp.dot(picked, couple_ref[...], preferred_element_type=F32)
+        before = sea_ref[pl.ds(i * 8, 8)].reshape(cells, chans).astype(F32)
+        keep(0, i, span, masked(span, before + forcing))
+
+    for k in range(2):
+        pk[k] = jnp.dot(pick_ref[...], st[k], preferred_element_type=F32).astype(BF)
+        last = grid_rows * grid_cols - edge
+        moves = [
+            (st.at[k, pl.ds(last, edge)], rn.at[k, 0], (f_next, t)),
+            (st.at[k, pl.ds(0, edge)], rn.at[k, 1], (f_prev, t)),
+            (pk.at[k, pl.ds(0, 96)], rw.at[k, pl.ds(0, 96)], (f, t_next)),
+            (pk.at[k, pl.ds(96, 96)], rw.at[k, pl.ds(96, 96)], (f, t_prev)),
+        ]
+        corner = 192
+        for fd in (f_prev, f_next):
+            for td in (t_prev, t_next):
+                part = pl.ds(corner, 16)
+                moves.append((pk.at[k, part], rw.at[k, part], (fd, td)))
+                corner += 16
+        copies = [
+            remote(src, dst, halo_send.at[k * 8 + j], halo_recv.at[k * 8 + j], device)
+            for j, (src, dst, device) in enumerate(moves)
+        ]
+        for copy in copies:
+            copy.start()
+        for copy in copies:
+            copy.wait_recv()
+        above, below, left, right = f > 0, f < n_f - 1, t > 0, t < 3
+
+        def valid(flag, values):
+            return jnp.where(flag, values.astype(F32), 0.0)
+
+        pd[0:3, 8 : 8 + grid_cols, :] = valid(above, rn[k, 0]).reshape(3, grid_cols, chans)
+        pd[3 + grid_rows : 6 + grid_rows, 8 : 8 + grid_cols, :] = valid(below, rn[k, 1]).reshape(
+            3, grid_cols, chans
+        )
+        flags = (
+            left,
+            right,
+            jnp.logical_and(below, right),
+            jnp.logical_and(below, left),
+            jnp.logical_and(above, right),
+            jnp.logical_and(above, left),
+        )
+        starts = (0, 96, 192, 208, 224, 240, 256)
+        came = jnp.concatenate(
+            [valid(flags[j], rw[k, starts[j] : starts[j + 1]]) for j in range(6)], axis=0
+        ).astype(BF)
+        strips = jnp.dot(place_ref[...], came, preferred_element_type=F32)
+        count = (grid_rows + 6) * 8
+        pd[:, 0:8, :] = strips[:count].reshape(grid_rows + 6, 8, chans)
+        pd[:, wide - 8 : wide, :] = strips[count:].reshape(grid_rows + 6, 8, chans)
+
+        @pl.loop(0, grid_rows + 6)
+        def _(r):
+            line = pd[r]
+            for b in range(7):
+                sh[b, r] = line[5 + b : 5 + b + grid_cols].reshape(grid_cols // 8, 8, chans)
+
+        @pl.loop(0, (grid_rows // 4) * (chans // 128))
+        def _(i):
+            first = (i // (chans // 128)) * 4
+            lanes = pl.ds(pl.multiple_of((i % (chans // 128)) * 128, 128), 128)
+            totals = [jnp.zeros((grid_cols // 8, 8, 128), F32) for _ in range(4)]
+            for b in range(7):
+                weights = [wb[k, a, b, :, lanes] for a in range(7)]
+                for r in range(10):
+                    values = sh[b, first + r, :, :, lanes]
+                    for j in range(4):
+                        if 0 <= r - j < 7:
+                            totals[j] = totals[j] + values * weights[r - j]
+            for j in range(4):
+                cv[first + j, :, :, lanes] = totals[j]
+
+        @pl.loop(0, grid_rows // 8)
+        def _(i):
+            span = pl.ds(pl.multiple_of(i * cells, cells), cells)
+            total = cv[pl.ds(i * 8, 8)].reshape(cells, chans)
+            center = total - jnp.mean(total, axis=-1, keepdims=True)
+            spread = jnp.mean(center * center, axis=-1, keepdims=True)
+            pnorm = (center * lax.rsqrt(spread + EPS) * sgain_ref[k : k + 1, :]).astype(BF)
+            inner = jax.nn.gelu(
+                jnp.dot(pnorm, one_ref[k], preferred_element_type=F32), approximate=True
+            ).astype(BF)
+            lowered = jnp.dot(inner, two_ref[k], preferred_element_type=F32)
+            values = masked(span, st[k, span, :].astype(F32) + lowered)
+            if k == 0:
+                keep(1, i, span, values)
+            else:
+                out_ref[pl.ds(i * 8, 8)] = values.reshape(8, grid_cols, chans)
+
+        for copy in copies:
+            copy.wait_send()
+
+
+def halo_matrices(grid_rows, grid_cols):
+    pick = np.zeros((256, grid_rows * grid_cols), np.float32)
+    place = np.zeros((2 * (grid_rows + 6) * 8, 256), np.float32)
+    side = (grid_rows + 6) * 8
+    for r in range(grid_rows):
+        for j in range(3):
+            pick[r * 3 + j, r * grid_cols + grid_cols - 3 + j] = 1
+            pick[96 + r * 3 + j, r * grid_cols + j] = 1
+            place[(3 + r) * 8 + 5 + j, r * 3 + j] = 1
+            place[side + (3 + r) * 8 + j, 96 + r * 3 + j] = 1
+    corner = 192
+    for down in (0, 1):
+        for right in (0, 1):
+            for i in range(3):
+                for j in range(3):
+                    row = grid_rows - 3 + i if down else i
+                    col = grid_cols - 3 + j if right else j
+                    pick[corner + i * 3 + j, row * grid_cols + col] = 1
+                    to_row = i if down else grid_rows + 3 + i
+                    to = to_row * 8 + 5 + j if right else side + to_row * 8 + j
+                    place[to, corner + i * 3 + j] = 1
+            corner += 16
+    return jnp.asarray(pick, BF), jnp.asarray(place, BF)
+
+
 def atmosphere_kernel(
     xs, zs,
     tok_ref, gain_ref, up_ref, down_ref, wfi_ref, wfo_ref,
-    atm_ref, win_ref,
+    sea_ref, mask_ref, map_ref, couple_ref, taps_ref, sgain_ref, one_ref, two_ref, pick_ref, place_ref,
+    atm_ref, out_ref,
     yb, gw, tk, nm, hd, fi, sb, rb, acc, at, ao, wn,
     y_send, y_recv, ring_send, ring_recv, tok_send, tok_recv, fi_send, fi_recv,
     rs_send, rs_recv, at_send, at_recv, fx_send, fx_recv, rim_send, rim_recv,
+    mk, oh, wb, st, pd, sh, cv, pk, rw, rn, halo_send, halo_recv,
 ):
     f = lax.axis_index("fsdp")
     t = lax.axis_index("tile")
@@ -48,14 +229,14 @@
     d_model = 4 * feat
 
     barrier = pltpu.get_barrier_semaphore()
-    for other in (yp, x_right, x_left, z_right, z_left):
+    for other in (x_right, x_left, z_right, z_left):
         pl.semaphore_signal(barrier, inc=1, device_id=(other, t), device_id_type=MESH)
     for other in (t_core, t_far, t_diag):
         pl.semaphore_signal(barrier, inc=1, device_id=(f, other), device_id_type=MESH)
-    pl.semaphore_signal(barrier, inc=1, device_id=(f_prev, 3), device_id_type=MESH)
-    pl.semaphore_signal(barrier, inc=1, device_id=(f_next, 0), device_id_type=MESH)
-    edge = jnp.where(jnp.logical_or(t == 0, t == 3), 4, 0)
-    pl.semaphore_wait(barrier, 8 + edge)
+    for other in (f_prev, f_next):
+        for q in range(4):
+            pl.semaphore_signal(barrier, inc=1, device_id=(other, q), device_id_type=MESH)
+    pl.semaphore_wait(barrier, 15)
 
     def remote(src, dst, send, recv, device):
         return pltpu.make_async_remote_copy(
@@ -174,6 +355,8 @@
             gain = gain_ref[:, q * feat : (q + 1) * feat]
             nm[span, q * feat : (q + 1) * feat] = (centers[q] * inverse * gain).astype(BF)
 
+    ocean_prepare(f * rows - quarter, mask_ref, map_ref, taps_ref, mk, oh, wb)
+
     for s in range(2, zs // 2):
         arrive(up_a)
         up_a = start(ring_round(0, 0, 1, s))
@@ -293,7 +476,10 @@
         copy.wait_recv()
     low[0].wait_recv()
     high[0].wait_recv()
-    win_ref[...] = wn[...]
+    ocean(
+        f, t, n_f, f_prev, f_next, remote, wn, sea_ref, couple_ref, sgain_ref, one_ref, two_ref,
+        pick_ref, place_ref, out_ref, mk, oh, wb, st, pd, sh, cv, pk, rw, rn, halo_send, halo_recv,
+    )
 
     @pl.when(t == 3)
     def _():
@@ -312,22 +498,41 @@
             copy.wait_send()
 
 
-def atmosphere(xs, zs, tokens, ln_gain, w_up, w_down, w_flux_in, w_flux_out):
+def body(
+    tokens,
+    ln_gain,
+    w_up,
+    w_down,
+    w_flux_in,
+    w_flux_out,
+    ocean_state,
+    land_mask,
+    column_map,
+    w_couple,
+    dw_kernel,
+    ocean_gain,
+    w_pw1,
+    w_pw2,
+):
+    xs, zs = XS, ZS
     rows, feat = tokens.shape
     d_model = 4 * feat
     shard, hidden = w_up.shape
     width = hidden // 4
     fh, flx = w_flux_out.shape
     quarter = rows // 4
+    grid_rows, grid_cols, chans = ocean_state.shape
+    cells = grid_rows * grid_cols
+    pick, place = halo_matrices(grid_rows, grid_cols)
     dma = pltpu.SemaphoreType.DMA
     vm = pl.BlockSpec(memory_space=pltpu.VMEM)
     return pl.pallas_call(
         functools.partial(atmosphere_kernel, xs, zs),
         out_shape=(
             jax.ShapeDtypeStruct((rows, feat), BF),
-            jax.ShapeDtypeStruct((6, quarter, flx), BF),
+            jax.ShapeDtypeStruct(ocean_state.shape, BF),
         ),
-        in_specs=[vm] * 6,
+        in_specs=[vm] * 16,
         out_specs=(vm, vm),
         scratch_shapes=[
             pltpu.VMEM((2, shard, hidden), BF),
@@ -346,92 +551,27 @@
             dma((3,)), dma((3,)), dma((3,)), dma((3,)),
             dma((6,)), dma((6,)), dma((3,)), dma((3,)),
             dma((3,)), dma((3,)), dma((4,)), dma((2,)),
+            pltpu.VMEM((cells, 128), F32),
+            pltpu.VMEM((cells, 6 * quarter), BF),
+            pltpu.VMEM((2, 7, 7, 8, chans), F32),
+            pltpu.VMEM((2, cells, chans), BF),
+            pltpu.VMEM((grid_rows + 6, grid_cols + 16, chans), F32),
+            pltpu.VMEM((7, grid_rows + 6, grid_cols // 8, 8, chans), F32),
+            pltpu.VMEM((grid_rows, grid_cols // 8, 8, chans), F32),
+            pltpu.VMEM((2, 256, chans), BF),
+            pltpu.VMEM((2, 256, chans), BF),
+            pltpu.VMEM((2, 2, 3 * grid_cols, chans), BF),
+            dma((16,)), dma((16,)),
         ],
         compiler_params=pltpu.CompilerParams(
-            collective_id=0, has_side_effects=True, vmem_limit_bytes=58 * 1024 * 1024
+            collective_id=0, has_side_effects=True, vmem_limit_bytes=60 * 1024 * 1024
         ),
-        name="atmosphere",
-    )(tokens, ln_gain.reshape(1, d_model), w_up, w_down.T, w_flux_in, w_flux_out)
-
-
-def with_halo(block, sides, width):
-    for axis, dim in sides:
-        count = lax.axis_size(axis)
-        forward = [(i, i + 1) for i in range(count - 1)]
-        backward = [(target, source) for source, target in forward]
-        low = lax.ppermute(
-            lax.slice_in_dim(block, block.shape[dim] - width, None, axis=dim), axis, forward
-        )
-        high = lax.ppermute(lax.slice_in_dim(block, 0, width, axis=dim), axis, backward)
-        block = jnp.concatenate([low, block, high], axis=dim)
-    return block
-
-
-def layer_norm(values, gain):
-    center = values - jnp.mean(values, axis=-1, keepdims=True)
-    spread = jnp.mean(center * center, axis=-1, keepdims=True)
-    return center * lax.rsqrt(spread + EPS) * gain
-
-
-def conv_block(padded, region_mask, kernel, gain, w_one, w_two):
-    rows = padded.shape[0] - 6
-    cols = padded.shape[1] - 6
-    chans = padded.shape[2]
-    total = jnp.zeros((rows, cols, chans), jnp.float32)
-    for first in range(7):
-        for second in range(7):
-            total = (
-                total
-                + padded[first : first + rows, second : second + cols].astype(jnp.float32)
-                * kernel[first, second]
-            )
-    pnorm = layer_norm(total, gain).astype(jnp.bfloat16).reshape(rows * cols, chans)
-    inner = jax.nn.gelu(
-        jnp.dot(pnorm, w_one, preferred_element_type=jnp.float32), approximate=True
-    ).astype(jnp.bfloat16)
-    lowered = jnp.dot(inner, w_two, preferred_element_type=jnp.float32).reshape(rows, cols, chans)
-    before = padded[3 : 3 + rows, 3 : 3 + cols].astype(jnp.float32)
-    return (region_mask[..., None] * (before + lowered)).astype(jnp.bfloat16)
-
-
-def body(
-    tokens,
-    ln_gain,
-    w_up,
-    w_down,
-    w_flux_in,
-    w_flux_out,
-    ocean_state,
-    land_mask,
-    column_map,
-    w_couple,
-    dw_kernel,
-    ocean_gain,
-    w_pw1,
-    w_pw2,
-):
-    band_rows = tokens.shape[0]
-    rim_rows = band_rows // 4
-    atm_out, window = atmosphere(XS, ZS, tokens, ln_gain, w_up, w_down, w_flux_in, w_flux_out)
-    window = window.reshape(6 * rim_rows, window.shape[-1])
-    band = lax.axis_index("fsdp")
-    local_index = (column_map - (band * band_rows - rim_rows)).reshape(-1)
-    picked = jnp.take(window, local_index, axis=0)
-    grid_rows = ocean_state.shape[0]
-    grid_cols = ocean_state.shape[1]
-    chans = ocean_state.shape[2]
-    forcing = jnp.dot(picked, w_couple, preferred_element_type=jnp.float32).reshape(
-        grid_rows, grid_cols, chans
+        name="coupled_step",
+    )(
+        tokens, ln_gain.reshape(1, d_model), w_up, w_down.T, w_flux_in, w_flux_out,
+        ocean_state, land_mask, column_map, w_couple, dw_kernel, ocean_gain, w_pw1, w_pw2,
+        pick, place,
     )
-    mask = land_mask.astype(jnp.float32)
-    state = (mask[..., None] * (ocean_state.astype(jnp.float32) + forcing)).astype(jnp.bfloat16)
-    count = dw_kernel.shape[0]
-    for block in range(count):
-        padded = with_halo(state, (("fsdp", 0), ("tile", 1)), 3)
-        state = conv_block(
-            padded, mask, dw_kernel[block], ocean_gain[block], w_pw1[block], w_pw2[block]
-        )
-    return (atm_out, state)
 
 
 def solution(mesh):

time: 201 us -> 166 us (0.83)
  the two profiles are of different devices: /device:TPU:3 before, /device:TPU:1 now
where the time goes in v2:
time: 166 us
  Pallas kernels  159 us (96%)
  local copies, waits for them, and re-layouts  5.79 us (3%)
    pallas_call x1, Pallas kernels, body(): pl.pallas_call(functools.partial(atmosphere_kernel, xs, zs), out_shape=(j...  159 us
    unnamed x5, local copies, waits for them, and re-layouts  4.5 us

profile of v2, /device:TPU:1, one launch (start us, length us, event | category | flops | bytes accessed | tf_op | source)
XLA Modules:
  0.0 165.8 jit_solution(4350591762525202894)
XLA Ops:
  0.6 1.3 reshape.7.gain_ref
  1.9 1.6 copy.18.taps_ref
  3.5 159.4 %coupled_step.1 = (bf16[1024,384]{1,0:T(8,128)(2,1)}, bf16[32,32,256]{2,1,0:T(8,128)(2,1)}) custom-call(bf16[1024,384]{1,0:T(8,128)(2,1)} %tok_ref.1, f32[1,1536]{1,0:T(1,128)} %reshape.7.gain_ref, bf16[24,1536]{1,0:T(8,128)(2,1)} %up_ref.1, bf16[24,1536]{1,0:T(8,128)(2,1)} %bitcast.1, bf16[384,768]{1,0:T(8,128)(2,1)} %wfi_ref.1, bf16[768,128]{1,0:T(8,128)(2,1)} %wfo_ref.1, ...), custom_call_target="tpu_custom_call" | custom-call | tf_op jit(solution)/shard_map/coupled_step/pallas_call | solution.py:529
  162.8 0.0 copy-start
  162.8 2.1 %copy.21 = bf16[1024,384]{1,0:T(8,128)(2,1)} copy(bf16[1024,384]{1,0:T(8,128)(2,1)} %get-tuple-element.4) | data formatting | bytes 1572864
  165.0 0.0 copy-done
  165.0 0.8 copy.22
Async XLA Ops:
  162.8 2.2 %copy-start = (bf16[32,32,256]{2,1,0:T(8,128)(2,1)S(1)}, bf16[32,32,256]{2,1,0:T(8,128)(2,1)}, u32[]{:S(2)}) copy-start(bf16[32,32,256]{2,1,0:T(8,128)(2,1)} %get-tuple-element.5) | copy-start | bytes 1572868

commit v3 on v2

--- a/solution.py
+++ b/solution.py
@@ -47,10 +47,10 @@
                 index_up == lane + 128.0 * k, 1.0, 0.0
             ).astype(BF)
 
-    for k in range(taps_ref.shape[0]):
+    for k in range(taps_ref.shape[2]):
         for a in range(7):
             for b in range(7):
-                wb[k, a, b] = jnp.broadcast_to(taps_ref[k, a, b : b + 1, :], wb.shape[3:])
+                wb[k, a, b] = jnp.broadcast_to(taps_ref[a, b, k : k + 1, :], wb.shape[3:])
 
 
 def ocean(
@@ -200,13 +200,15 @@
 
 def atmosphere_kernel(
     xs, zs,
-    tok_ref, gain_ref, up_ref, down_ref, wfi_ref, wfo_ref,
-    sea_ref, mask_ref, map_ref, couple_ref, taps_ref, sgain_ref, one_ref, two_ref, pick_ref, place_ref,
+    tok_ref, gain_ref, up_ref, down_ref, wfi_ref, wfo_hbm,
+    sea_hbm, mask_ref, map_ref, couple_hbm, taps_ref, sgain_ref, one_hbm, two_hbm, pick_hbm, place_hbm,
     atm_ref, out_ref,
     yb, gw, tk, nm, hd, fi, sb, rb, acc, at, ao, wn,
     y_send, y_recv, ring_send, ring_recv, tok_send, tok_recv, fi_send, fi_recv,
     rs_send, rs_recv, at_send, at_recv, fx_send, fx_recv, rim_send, rim_recv,
     mk, oh, wb, st, pd, sh, cv, pk, rw, rn, halo_send, halo_recv,
+    wfo_ref, sea_ref, couple_ref, one_ref, two_ref, pick_ref, place_ref, load_sem,
+    tok_hop, fi_hop, rs_hop, hop_send, hop_recv,
 ):
     f = lax.axis_index("fsdp")
     t = lax.axis_index("tile")
@@ -236,6 +238,16 @@
     for other in (f_prev, f_next):
         for q in range(4):
             pl.semaphore_signal(barrier, inc=1, device_id=(other, q), device_id_type=MESH)
+    tok_load = pltpu.make_async_copy(tok_ref, tk.at[t], load_sem.at[0])
+    fi_load = pltpu.make_async_copy(wfi_ref, fi.at[t], load_sem.at[1])
+    loads = [
+        pltpu.make_async_copy(src, dst, load_sem.at[2 + j])
+        for j, (src, dst) in enumerate((
+            (wfo_hbm, wfo_ref), (sea_hbm, sea_ref), (couple_hbm, couple_ref), (one_hbm, one_ref),
+            (two_hbm, two_ref), (pick_hbm, pick_ref), (place_hbm, place_ref),
+        ))
+    ]
+    tok_load.start()
     pl.semaphore_wait(barrier, 15)
 
     def remote(src, dst, send, recv, device):
@@ -250,15 +262,41 @@
     ]
     for copy in y_copies:
         copy.start()
-    shared = []
-    for src, dst, send, recv in ((tok_ref, tk, tok_send, tok_recv), (wfi_ref, fi, fi_send, fi_recv)):
-        far = remote(src, dst.at[t], send.at[1], recv.at[1], (f, t_far))
-        near = remote(src, dst.at[t], send.at[0], recv.at[0], (f, t_core))
-        relay = remote(dst.at[t_far], dst.at[t_far], send.at[2], recv.at[2], (f, t_core))
-        shared.append((near, far, relay))
-    for near, far, relay in shared:
-        far.start()
-        near.start()
+    y_at = yh * 2 + yl
+    y_ways = []
+    for way in (1, 3):
+        y_to = (y_at + way) % 4
+        y_ways.append((f - yl + y_to % 2, (y_to // 2) * 2 + c))
+
+    def far_out(src, hop, sem):
+        return [
+            remote(src[h], hop.at[h], hop_send.at[sem + h], hop_recv.at[sem + h], y_ways[h])
+            for h in (0, 1)
+        ]
+
+    def far_on(hop, dst, sem):
+        copies = []
+        for h in (0, 1):
+            origin = (1 - y_ways[h][1] // 2) * 2 + c
+            copies.append(
+                remote(
+                    hop.at[h], dst(origin, h), hop_send.at[sem + 2 + h], hop_recv.at[sem + 2 + h],
+                    y_ways[h],
+                )
+            )
+        return copies
+
+    half_rows, half_feat = rows // 2, feat // 2
+    tok_parts = [pl.ds(h * half_rows, half_rows) for h in (0, 1)]
+    fi_parts = [pl.ds(h * half_feat, half_feat) for h in (0, 1)]
+    tok_out = far_out([tok_ref.at[part] for part in tok_parts], tok_hop, 0)
+    tok_on = far_on(tok_hop, lambda q, h: tk.at[q, tok_parts[h]], 0)
+    fi_out = far_out([wfi_ref.at[part] for part in fi_parts], fi_hop, 4)
+    fi_on = far_on(fi_hop, lambda q, h: fi.at[q, fi_parts[h]], 4)
+    tok_near = remote(tok_ref, tk.at[t], tok_send.at[0], tok_recv.at[0], (f, t_core))
+    fi_near = remote(wfi_ref, fi.at[t], fi_send.at[0], fi_recv.at[0], (f, t_core))
+    tok_relay = remote(tk.at[t_far], tk.at[t_far], tok_send.at[1], tok_recv.at[1], (f, t_core))
+    fi_relay = remote(fi.at[t_far], fi.at[t_far], fi_send.at[1], fi_recv.at[1], (f, t_core))
 
     def ring_round(w, stream, stage, s):
         on_x = (stream == 0) == (stage == 0)
@@ -298,7 +336,11 @@
         for copy in copies:
             copy.wait_recv()
 
-    for w, ref in enumerate((up_ref, down_ref)):
+    def advance(old, w, stream, stage, s):
+        arrive(old)
+        return start(ring_round(w, stream, stage, s))
+
+    def assemble(w, ref):
         y_copies[w].wait_recv()
         for p in range(4):
             mine = ref[:, p * width : (p + 1) * width].astype(F32)
@@ -306,41 +348,39 @@
             first = jnp.where(yl == 0, mine, other)
             second = jnp.where(yl == 0, other, mine)
             gw[w, p, x, z] = jnp.concatenate([first, second], axis=0).astype(BF)
-        if w == 0:
-            up_small = [start(ring_round(0, b, 0, 0)) for b in (0, 1)]
-    down_small = [start(ring_round(1, b, 0, 0)) for b in (0, 1)]
-    tk[t] = tok_ref[...]
-    fi[t] = wfi_ref[...]
-
-    sizes = (xs // 2, zs // 2)
-    for s in range(1, max(sizes)):
-        for w, small in ((0, up_small), (1, down_small)):
-            for b in (0, 1):
-                if s < sizes[b]:
-                    arrive(small[b])
-                    small[b] = start(ring_round(w, b, 0, s))
-    arrive(up_small[0])
-    up_a = start(ring_round(0, 0, 1, 0))
-    arrive(up_small[1])
-    up_b = start(ring_round(0, 1, 1, 0))
-    arrive(down_small[0])
-    down_a = start(ring_round(1, 0, 1, 0))
-    arrive(down_small[1])
-    down_b = start(ring_round(1, 1, 1, 0))
-
-    for near, far, relay in shared:
-        far.wait_recv()
-        relay.start()
-
-    arrive(up_a)
-    up_a = start(ring_round(0, 0, 1, 1)) if zs // 2 > 1 else []
-    arrive(up_b)
-    up_b = start(ring_round(0, 1, 1, 1)) if xs // 2 > 1 else []
-    arrive(down_a)
-    down_a = start(ring_round(1, 0, 1, 1)) if zs // 2 > 1 else []
-
-    shared[0][0].wait_recv()
-    shared[0][2].wait_recv()
+
+    for copy in tok_out:
+        copy.start()
+    tok_near.start()
+    for copy in loads:
+        copy.start()
+    fi_load.start()
+    assemble(0, up_ref)
+    up_b = start(ring_round(0, 1, 0, 0))
+    up_a = start(ring_round(0, 0, 0, 0))
+    assemble(1, down_ref)
+    up_a = advance(up_a, 0, 0, 0, 1)
+    up_b = advance(up_b, 0, 1, 0, 1)
+    down_b = start(ring_round(1, 1, 0, 0))
+    up_b = advance(up_b, 0, 1, 0, 2)
+    up_a = advance(up_a, 0, 0, 1, 0)
+    arrive(tok_out)
+    start(tok_on)
+    up_b = advance(up_b, 0, 1, 0, 3)
+    down_a = start(ring_round(1, 0, 0, 0))
+    down_b = advance(down_b, 1, 1, 0, 1)
+    up_b = advance(up_b, 0, 1, 1, 0)
+    down_a = advance(down_a, 1, 0, 0, 1)
+    down_b = advance(down_b, 1, 1, 0, 2)
+    up_a = advance(up_a, 0, 0, 1, 1)
+    arrive(tok_on)
+    start([tok_relay])
+    start(fi_out)
+    start([fi_near])
+    down_b = advance(down_b, 1, 1, 0, 3)
+    tok_load.wait()
+    tok_near.wait_recv()
+    tok_relay.wait_recv()
     step = min(32, quarter)
 
     @pl.loop(0, rows // step)
@@ -352,28 +392,22 @@
         spread = sum(jnp.sum(v * v, axis=-1, keepdims=True) for v in centers) / d_model
         inverse = lax.rsqrt(spread + EPS)
         for q in range(4):
-            gain = gain_ref[:, q * feat : (q + 1) * feat]
+            gain = gain_ref[q * feat : (q + 1) * feat][None, :]
             nm[span, q * feat : (q + 1) * feat] = (centers[q] * inverse * gain).astype(BF)
 
+    up_a = advance(up_a, 0, 0, 1, 2)
+    up_b = advance(up_b, 0, 1, 1, 1)
     ocean_prepare(f * rows - quarter, mask_ref, map_ref, taps_ref, mk, oh, wb)
-
-    for s in range(2, zs // 2):
-        arrive(up_a)
-        up_a = start(ring_round(0, 0, 1, s))
-        if s == 2:
-            arrive(down_b)
-            down_b = start(ring_round(1, 1, 1, 1)) if xs // 2 > 1 else []
-        arrive(down_a)
-        down_a = start(ring_round(1, 0, 1, s))
-    if zs // 2 <= 2 and xs // 2 > 1:
-        arrive(down_b)
-        down_b = start(ring_round(1, 1, 1, 1))
+    up_a = advance(up_a, 0, 0, 1, 3)
+    down_a = advance(down_a, 1, 0, 1, 0)
+    arrive(fi_out)
+    start(fi_on)
     arrive(up_b)
+    down_b = advance(down_b, 1, 1, 1, 0)
     arrive(up_a)
-
-    @pl.loop(0, 8)
-    def _(i):
-        half, block = i // 4, i % 4
+    down_a = advance(down_a, 1, 0, 1, 1)
+
+    def up_block(half, block):
         span = pl.ds(pl.multiple_of(block * quarter, quarter), quarter)
         rhs = jnp.concatenate(
             [gw[0, half * 2 + k].reshape(d_model, width) for k in (0, 1)], axis=1
@@ -381,6 +415,17 @@
         pre = jnp.dot(nm[span, :], rhs, preferred_element_type=F32)
         hd[half, span, :] = jax.nn.gelu(pre, approximate=True).astype(BF)
 
+    for half in (0, 1):
+        @pl.loop(0, 4)
+        def _(block):
+            up_block(half, block)
+
+        if half == 0:
+            down_a = advance(down_a, 1, 0, 1, 2)
+            down_b = advance(down_b, 1, 1, 1, 1)
+            arrive(fi_on)
+            start([fi_relay])
+    down_a = advance(down_a, 1, 0, 1, 3)
     arrive(down_b)
     arrive(down_a)
 
@@ -400,7 +445,8 @@
         )
 
     to_core = [sums(0, half, t_core) for half in (0, 1)]
-    to_far = [sums(1, half, t_far) for half in (0, 1)]
+    far_sums = far_out([sb.at[1, half] for half in (0, 1)], rs_hop, 8)
+    far_sums_on = far_on(rs_hop, lambda q, half: rb.at[1, half], 8)
     to_core2 = [sums(2, half, t_core) for half in (0, 1)]
 
     for half in (0, 1):
@@ -410,16 +456,18 @@
         acc[half] = partial(t_far, half)
         to_core[half].wait_recv()
         sb[1, half] = (acc[half] + rb[0, half].astype(F32)).astype(BF)
-        to_far[half].start()
+        far_sums[half].start()
     for half in (0, 1):
         sb[2, half] = partial(t_core, half).astype(BF)
         to_core2[half].start()
     for half in (0, 1):
         acc[half] = partial(t, half)
+    arrive(far_sums)
+    start(far_sums_on)
     mine = pl.ds(pl.multiple_of(t * quarter, quarter), quarter)
     for half in (0, 1):
         to_core2[half].wait_recv()
-        to_far[half].wait_recv()
+        far_sums_on[half].wait_recv()
         for k in (0, 1):
             q = 2 * half + k
             cols = slice(k * feat, (k + 1) * feat)
@@ -433,8 +481,11 @@
         at_copies[-1].start()
     ao[t] = at[t]
 
-    shared[1][0].wait_recv()
-    shared[1][2].wait_recv()
+    fi_load.wait()
+    fi_near.wait_recv()
+    fi_relay.wait_recv()
+    for copy in loads:
+        copy.wait()
     pre = jnp.dot(
         jnp.concatenate([at[q] for q in range(4)], axis=1),
         fi[...].reshape(d_model, fi.shape[-1]),
@@ -491,11 +542,8 @@
         for copy in high:
             copy.wait_send()
 
-    for copy in y_copies + done + at_copies + fx_copies + to_core + to_far + to_core2:
+    for copy in y_copies + done + tok_out + [tok_near] + at_copies + fx_copies + to_core + far_sums + to_core2:
         copy.wait_send()
-    for trio in shared:
-        for copy in trio:
-            copy.wait_send()
 
 
 def body(
@@ -526,13 +574,14 @@
     pick, place = halo_matrices(grid_rows, grid_cols)
     dma = pltpu.SemaphoreType.DMA
     vm = pl.BlockSpec(memory_space=pltpu.VMEM)
+    hb = pl.BlockSpec(memory_space=pl.ANY)
     return pl.pallas_call(
         functools.partial(atmosphere_kernel, xs, zs),
         out_shape=(
             jax.ShapeDtypeStruct((rows, feat), BF),
             jax.ShapeDtypeStruct(ocean_state.shape, BF),
         ),
-        in_specs=[vm] * 16,
+        in_specs=[hb, vm, vm, vm, hb, hb, hb, vm, vm, hb, vm, vm, hb, hb, hb, hb],
         out_specs=(vm, vm),
         scratch_shapes=[
             pltpu.VMEM((2, shard, hidden), BF),
@@ -562,14 +611,26 @@
             pltpu.VMEM((2, 256, chans), BF),
             pltpu.VMEM((2, 2, 3 * grid_cols, chans), BF),
             dma((16,)), dma((16,)),
+            pltpu.VMEM(w_flux_out.shape, BF),
+            pltpu.VMEM(ocean_state.shape, BF),
+            pltpu.VMEM(w_couple.shape, BF),
+            pltpu.VMEM(w_pw1.shape, BF),
+            pltpu.VMEM(w_pw2.shape, BF),
+            pltpu.VMEM(pick.shape, BF),
+            pltpu.VMEM(place.shape, BF),
+            dma((9,)),
+            pltpu.VMEM((2, rows // 2, feat), BF),
+            pltpu.VMEM((2, feat // 2, fh), BF),
+            pltpu.VMEM((2, quarter, d_model // 2), BF),
+            dma((12,)), dma((12,)),
         ],
         compiler_params=pltpu.CompilerParams(
             collective_id=0, has_side_effects=True, vmem_limit_bytes=60 * 1024 * 1024
         ),
         name="coupled_step",
     )(
-        tokens, ln_gain.reshape(1, d_model), w_up, w_down.T, w_flux_in, w_flux_out,
-        ocean_state, land_mask, column_map, w_couple, dw_kernel, ocean_gain, w_pw1, w_pw2,
+        tokens, ln_gain, w_up, w_down.T, w_flux_in, w_flux_out,
+        ocean_state, land_mask, column_map, w_couple, dw_kernel.transpose(1, 2, 0, 3), ocean_gain, w_pw1, w_pw2,
         pick, place,
     )
 

time: 166 us -> 169 us (1.018)
  Pallas kernels: 159 us -> 164 us
  local copies, waits for them, and re-layouts: 5.79 us -> 2.95 us
    pallas_call x1, Pallas kernels: 159 us -> 164 us  [body(): pl.pallas_call(functools.partial(atmosphere_kernel, xs, zs), out_shape=(j...]
    unnamed x5 -> x4, local copies, waits for them, and re-layouts: 4.5 us -> 2.95 us
where the time goes in v3:
time: 169 us; the launch traced here: 167 us
  Pallas kernels  164 us (97%)
  local copies, waits for them, and re-layouts  2.95 us (2%)
    pallas_call x1, Pallas kernels, body(): pl.pallas_call(functools.partial(atmosphere_kernel, xs, zs), out_shape=(j...  164 us

profile of v3, /device:TPU:1, one launch (start us, length us, event | category | flops | bytes accessed | tf_op | source)
XLA Modules:
  0.0 167.1 jit_solution(9719040677388682958)
XLA Ops:
  0.6 163.5 %coupled_step.1 = (bf16[1024,384]{1,0:T(8,128)(2,1)}, bf16[32,32,256]{2,1,0:T(8,128)(2,1)}) custom-call(bf16[1024,384]{1,0:T(8,128)(2,1)} %tok_ref.1, f32[1536]{0:T(1024)} %gain_ref.1, bf16[24,1536]{1,0:T(8,128)(2,1)} %up_ref.1, bf16[24,1536]{1,0:T(8,128)(2,1)} %bitcast.3, bf16[384,768]{1,0:T(8,128)(2,1)} %wfi_ref.1, bf16[768,128]{1,0:T(8,128)(2,1)} %wfo_hbm.1, ...), custom_call_target="tpu_custom_call" | custom-call | tf_op jit(solution)/shard_map/coupled_step/pallas_call | solution.py:578
  164.2 0.0 copy-start
  164.2 2.1 %copy.20 = bf16[1024,384]{1,0:T(8,128)(2,1)} copy(bf16[1024,384]{1,0:T(8,128)(2,1)} %get-tuple-element.4) | data formatting | bytes 1572864
  166.3 0.0 copy-done
  166.3 0.8 copy.21
Async XLA Ops:
  164.2 2.2 %copy-start = (bf16[32,32,256]{2,1,0:T(8,128)(2,1)S(1)}, bf16[32,32,256]{2,1,0:T(8,128)(2,1)}, u32[]{:S(2)}) copy-start(bf16[32,32,256]{2,1,0:T(8,128)(2,1)} %get-tuple-element.5) | copy-start | bytes 1572868

commit v4 on v3

--- a/solution.py
+++ b/solution.py
@@ -55,7 +55,7 @@
 
 def ocean(
     f, t, n_f, f_prev, f_next, remote, wn, sea_ref, couple_ref, sgain_ref, one_ref, two_ref,
-    pick_ref, place_ref, out_ref, mk, oh, wb, st, pd, sh, cv, pk, rw, rn, halo_send, halo_recv,
+    pick_ref, place_ref, out_ref, mk, oh, wb, st, pd, sh, cv, pk, rw, rn, halo_send, halo_recv, at_copies,
 ):
     grid_rows, grid_cols, chans = sea_ref.shape
     cells = 8 * grid_cols
@@ -105,6 +105,9 @@
             copy.start()
         for copy in copies:
             copy.wait_recv()
+        if k == 0:
+            for copy in at_copies:
+                copy.start()
         above, below, left, right = f > 0, f < n_f - 1, t > 0, t < 3
 
         def valid(flag, values):
@@ -303,25 +306,25 @@
         n = xs if on_x else zs
         here = x if on_x else z
         last = s == n // 2 - 1
-        copies = []
-        for way in (0, 1):
-            chunk = (here - s + n) % n if way == 0 else (here + s) % n
-            if last:
-                pieces = 2 * stream + way
-            else:
-                pieces = pl.ds(2 * stream, 2)
-            if stage == 0:
-                part = gw.at[w, pieces, chunk, z] if on_x else gw.at[w, pieces, x, chunk]
-            else:
-                part = gw.at[w, pieces, chunk] if on_x else gw.at[w, pieces, :, chunk]
-            if on_x:
-                target = x_right if way == 0 else x_left
-            else:
-                target = z_right if way == 0 else z_left
-            at_sem = (((w * 2 + stream) * 2 + stage) * 4 + s) * 2 + way
-            copies.append(
-                remote(part, part, ring_send.at[at_sem], ring_recv.at[at_sem], (target, t))
-            )
+        copies = [[], []]
+        for k in (0, 1):
+            piece = 2 * stream + k
+            for way in (0, 1):
+                if last and way != k:
+                    continue
+                chunk = (here - s + n) % n if way == 0 else (here + s) % n
+                if stage == 0:
+                    part = gw.at[w, piece, chunk, z] if on_x else gw.at[w, piece, x, chunk]
+                else:
+                    part = gw.at[w, piece, chunk] if on_x else gw.at[w, piece, :, chunk]
+                if on_x:
+                    target = x_right if way == 0 else x_left
+                else:
+                    target = z_right if way == 0 else z_left
+                at_sem = ((((w * 2 + stream) * 2 + stage) * 4 + s) * 2 + way) * 2 + k
+                copies[k].append(
+                    remote(part, part, ring_send.at[at_sem], ring_recv.at[at_sem], (target, t))
+                )
         return copies
 
     done = []
@@ -336,9 +339,17 @@
         for copy in copies:
             copy.wait_recv()
 
+    def begin(w, stream):
+        new = ring_round(w, stream, 0, 0)
+        start(new[0] + new[1])
+        return new
+
     def advance(old, w, stream, stage, s):
-        arrive(old)
-        return start(ring_round(w, stream, stage, s))
+        new = ring_round(w, stream, stage, s)
+        for k in (0, 1):
+            arrive(old[k])
+            start(new[k])
+        return new
 
     def assemble(w, ref):
         y_copies[w].wait_recv()
@@ -356,18 +367,18 @@
         copy.start()
     fi_load.start()
     assemble(0, up_ref)
-    up_b = start(ring_round(0, 1, 0, 0))
-    up_a = start(ring_round(0, 0, 0, 0))
+    up_b = begin(0, 1)
+    up_a = begin(0, 0)
     assemble(1, down_ref)
     up_a = advance(up_a, 0, 0, 0, 1)
     up_b = advance(up_b, 0, 1, 0, 1)
-    down_b = start(ring_round(1, 1, 0, 0))
+    down_b = begin(1, 1)
     up_b = advance(up_b, 0, 1, 0, 2)
     up_a = advance(up_a, 0, 0, 1, 0)
     arrive(tok_out)
     start(tok_on)
     up_b = advance(up_b, 0, 1, 0, 3)
-    down_a = start(ring_round(1, 0, 0, 0))
+    down_a = begin(1, 0)
     down_b = advance(down_b, 1, 1, 0, 1)
     up_b = advance(up_b, 0, 1, 1, 0)
     down_a = advance(down_a, 1, 0, 0, 1)
@@ -402,9 +413,9 @@
     down_a = advance(down_a, 1, 0, 1, 0)
     arrive(fi_out)
     start(fi_on)
-    arrive(up_b)
+    arrive(up_b[0] + up_b[1])
     down_b = advance(down_b, 1, 1, 1, 0)
-    arrive(up_a)
+    arrive(up_a[0] + up_a[1])
     down_a = advance(down_a, 1, 0, 1, 1)
 
     def up_block(half, block):
@@ -426,8 +437,8 @@
             arrive(fi_on)
             start([fi_relay])
     down_a = advance(down_a, 1, 0, 1, 3)
-    arrive(down_b)
-    arrive(down_a)
+    arrive(down_b[0] + down_b[1])
+    arrive(down_a[0] + down_a[1])
 
     def partial(block, half):
         span = pl.ds(pl.multiple_of(block * quarter, quarter), quarter)
@@ -478,7 +489,6 @@
     for k in range(1, 4):
         q = (t + k) % 4
         at_copies.append(remote(at.at[q], ao.at[t], at_send.at[k - 1], at_recv.at[k - 1], (f, q)))
-        at_copies[-1].start()
     ao[t] = at[t]
 
     fi_load.wait()
@@ -519,18 +529,18 @@
         for copy in high:
             copy.start()
 
-    for copy in at_copies:
-        copy.wait_recv()
-    for q in range(4):
-        atm_ref[pl.ds(q * quarter, quarter), :] = ao[q]
     for copy in fx_copies:
         copy.wait_recv()
     low[0].wait_recv()
     high[0].wait_recv()
     ocean(
         f, t, n_f, f_prev, f_next, remote, wn, sea_ref, couple_ref, sgain_ref, one_ref, two_ref,
-        pick_ref, place_ref, out_ref, mk, oh, wb, st, pd, sh, cv, pk, rw, rn, halo_send, halo_recv,
+        pick_ref, place_ref, out_ref, mk, oh, wb, st, pd, sh, cv, pk, rw, rn, halo_send, halo_recv, at_copies,
     )
+    for copy in at_copies:
+        copy.wait_recv()
+    for q in range(4):
+        atm_ref[pl.ds(q * quarter, quarter), :] = ao[q]
 
     @pl.when(t == 3)
     def _():
@@ -596,7 +606,7 @@
             pltpu.VMEM((4, quarter, feat), BF),
             pltpu.VMEM((4, quarter, feat), BF),
             pltpu.VMEM((6, quarter, flx), BF),
-            dma((2,)), dma((2,)), dma((64,)), dma((64,)),
+            dma((2,)), dma((2,)), dma((128,)), dma((128,)),
             dma((3,)), dma((3,)), dma((3,)), dma((3,)),
             dma((6,)), dma((6,)), dma((3,)), dma((3,)),
             dma((3,)), dma((3,)), dma((4,)), dma((2,)),

time: 169 us -> 157 us (0.929); the launches traced: 167 us -> 157 us
  Pallas kernels: 164 us -> 154 us
    pallas_call x1, Pallas kernels: 164 us -> 154 us  [body(): pl.pallas_call(functools.partial(atmosphere_kernel, xs, zs), out_shape=(j...]
where the time goes in v4:
time: 157 us
  Pallas kernels  154 us (98%)
  local copies, waits for them, and re-layouts  2.95 us (2%)
    pallas_call x1, Pallas kernels, body(): pl.pallas_call(functools.partial(atmosphere_kernel, xs, zs), out_shape=(j...  154 us

profile of v4, /device:TPU:1, one launch (start us, length us, event | category | flops | bytes accessed | tf_op | source)
XLA Modules:
  0.0 157.4 jit_solution(18435909455660435753)
XLA Ops:
  0.6 153.8 %coupled_step.1 = (bf16[1024,384]{1,0:T(8,128)(2,1)}, bf16[32,32,256]{2,1,0:T(8,128)(2,1)}) custom-call(bf16[1024,384]{1,0:T(8,128)(2,1)} %tok_ref.1, f32[1536]{0:T(1024)} %gain_ref.1, bf16[24,1536]{1,0:T(8,128)(2,1)} %up_ref.1, bf16[24,1536]{1,0:T(8,128)(2,1)} %bitcast.3, bf16[384,768]{1,0:T(8,128)(2,1)} %wfi_ref.1, bf16[768,128]{1,0:T(8,128)(2,1)} %wfo_hbm.1, ...), custom_call_target="tpu_custom_call" | custom-call | tf_op jit(solution)/shard_map/coupled_step/pallas_call | solution.py:588
  154.4 0.0 copy-start
  154.4 2.1 %copy.20 = bf16[1024,384]{1,0:T(8,128)(2,1)} copy(bf16[1024,384]{1,0:T(8,128)(2,1)} %get-tuple-element.4) | data formatting | bytes 1572864
  156.6 0.0 copy-done
  156.6 0.8 copy.21
Async XLA Ops:
  154.4 2.2 %copy-start = (bf16[32,32,256]{2,1,0:T(8,128)(2,1)S(1)}, bf16[32,32,256]{2,1,0:T(8,128)(2,1)}, u32[]{:S(2)}) copy-start(bf16[32,32,256]{2,1,0:T(8,128)(2,1)} %get-tuple-element.5) | copy-start | bytes 1572868

commit v5 on v4

--- a/solution.py
+++ b/solution.py
@@ -14,6 +14,7 @@
 EPS = 1e-06
 XS = 4
 ZS = 8
+FIRST = 32
 
 
 def nt_dot(lhs, rhs):
@@ -176,6 +177,18 @@
             copy.wait_send()
 
 
+def order_matrix(group, count):
+    matrix = np.zeros((group * count, group * count), np.float32)
+    for k in range(count):
+        for i in range(group):
+            if i < FIRST:
+                to = k * FIRST + i
+            else:
+                to = count * FIRST + k * (group - FIRST) + i - FIRST
+            matrix[k * group + i, to] = 1
+    return jnp.asarray(matrix, BF)
+
+
 def halo_matrices(grid_rows, grid_cols):
     pick = np.zeros((256, grid_rows * grid_cols), np.float32)
     place = np.zeros((2 * (grid_rows + 6) * 8, 256), np.float32)
@@ -204,14 +217,14 @@
 def atmosphere_kernel(
     xs, zs,
     tok_ref, gain_ref, up_ref, down_ref, wfi_ref, wfo_hbm,
-    sea_hbm, mask_ref, map_ref, couple_hbm, taps_ref, sgain_ref, one_hbm, two_hbm, pick_hbm, place_hbm,
+    sea_hbm, mask_ref, map_ref, couple_hbm, taps_ref, sgain_ref, one_hbm, two_hbm, pick_hbm, place_hbm, order_hbm,
     atm_ref, out_ref,
-    yb, gw, tk, nm, hd, fi, sb, rb, acc, at, ao, wn,
+    yb, gw, gd0, gd1, tk, nm, hd, fi, sb0, sb1, rb0, rb1, acc0, acc1, tp, order_ref, at, ao, wn,
     y_send, y_recv, ring_send, ring_recv, tok_send, tok_recv, fi_send, fi_recv,
     rs_send, rs_recv, at_send, at_recv, fx_send, fx_recv, rim_send, rim_recv,
     mk, oh, wb, st, pd, sh, cv, pk, rw, rn, halo_send, halo_recv,
     wfo_ref, sea_ref, couple_ref, one_ref, two_ref, pick_ref, place_ref, load_sem,
-    tok_hop, fi_hop, rs_hop, hop_send, hop_recv,
+    tok_hop, fi_hop, rs_hop0, rs_hop1, hop_send, hop_recv,
 ):
     f = lax.axis_index("fsdp")
     t = lax.axis_index("tile")
@@ -231,6 +244,7 @@
     quarter = rows // 4
     feat = tok_ref.shape[1]
     width = gw.shape[-1]
+    weights = (gw, gd0, gd1)
     d_model = 4 * feat
 
     barrier = pltpu.get_barrier_semaphore()
@@ -248,6 +262,7 @@
         for j, (src, dst) in enumerate((
             (wfo_hbm, wfo_ref), (sea_hbm, sea_ref), (couple_hbm, couple_ref), (one_hbm, one_ref),
             (two_hbm, two_ref), (pick_hbm, pick_ref), (place_hbm, place_ref),
+            (order_hbm, order_ref),
         ))
     ]
     tok_load.start()
@@ -314,9 +329,9 @@
                     continue
                 chunk = (here - s + n) % n if way == 0 else (here + s) % n
                 if stage == 0:
-                    part = gw.at[w, piece, chunk, z] if on_x else gw.at[w, piece, x, chunk]
+                    part = weights[w].at[piece, chunk, z] if on_x else weights[w].at[piece, x, chunk]
                 else:
-                    part = gw.at[w, piece, chunk] if on_x else gw.at[w, piece, :, chunk]
+                    part = weights[w].at[piece, chunk] if on_x else weights[w].at[piece, :, chunk]
                 if on_x:
                     target = x_right if way == 0 else x_left
                 else:
@@ -358,7 +373,12 @@
             other = yb[w, :, p * width : (p + 1) * width].astype(F32)
             first = jnp.where(yl == 0, mine, other)
             second = jnp.where(yl == 0, other, mine)
-            gw[w, p, x, z] = jnp.concatenate([first, second], axis=0).astype(BF)
+            both = jnp.concatenate([first, second], axis=0).astype(BF)
+            if w == 0:
+                gw[p, x, z] = both
+            else:
+                gd0[p, x, z] = both[:FIRST]
+                gd1[p, x, z] = both[FIRST:]
 
     for copy in tok_out:
         copy.start()
@@ -379,16 +399,20 @@
     start(tok_on)
     up_b = advance(up_b, 0, 1, 0, 3)
     down_a = begin(1, 0)
+    last_a = begin(2, 0)
     down_b = advance(down_b, 1, 1, 0, 1)
     up_b = advance(up_b, 0, 1, 1, 0)
     down_a = advance(down_a, 1, 0, 0, 1)
     down_b = advance(down_b, 1, 1, 0, 2)
     up_a = advance(up_a, 0, 0, 1, 1)
+    last_b = begin(2, 1)
+    last_a = advance(last_a, 2, 0, 0, 1)
     arrive(tok_on)
     start([tok_relay])
     start(fi_out)
     start([fi_near])
     down_b = advance(down_b, 1, 1, 0, 3)
+    last_b = advance(last_b, 2, 1, 0, 1)
     tok_load.wait()
     tok_near.wait_recv()
     tok_relay.wait_recv()
@@ -408,8 +432,15 @@
 
     up_a = advance(up_a, 0, 0, 1, 2)
     up_b = advance(up_b, 0, 1, 1, 1)
+    last_b = advance(last_b, 2, 1, 0, 2)
+    loads[-1].wait()
+    mine = pl.ds(pl.multiple_of(t * quarter, quarter), quarter)
+    for half in (0, 1):
+        natural = jnp.concatenate([tk[2 * half + k, mine, :] for k in (0, 1)], axis=1)
+        tp[half] = jnp.dot(natural, order_ref[...], preferred_element_type=F32).astype(BF)
     ocean_prepare(f * rows - quarter, mask_ref, map_ref, taps_ref, mk, oh, wb)
     up_a = advance(up_a, 0, 0, 1, 3)
+    last_b = advance(last_b, 2, 1, 0, 3)
     down_a = advance(down_a, 1, 0, 1, 0)
     arrive(fi_out)
     start(fi_on)
@@ -421,7 +452,7 @@
     def up_block(half, block):
         span = pl.ds(pl.multiple_of(block * quarter, quarter), quarter)
         rhs = jnp.concatenate(
-            [gw[0, half * 2 + k].reshape(d_model, width) for k in (0, 1)], axis=1
+            [gw[half * 2 + k].reshape(d_model, width) for k in (0, 1)], axis=1
         )
         pre = jnp.dot(nm[span, :], rhs, preferred_element_type=F32)
         hd[half, span, :] = jax.nn.gelu(pre, approximate=True).astype(BF)
@@ -438,52 +469,78 @@
             start([fi_relay])
     down_a = advance(down_a, 1, 0, 1, 3)
     arrive(down_b[0] + down_b[1])
+    last_b = advance(last_b, 2, 1, 1, 0)
     arrive(down_a[0] + down_a[1])
-
-    def partial(block, half):
+    last_a = advance(last_a, 2, 0, 1, 0)
+
+    def partial(j, block, half):
         span = pl.ds(pl.multiple_of(block * quarter, quarter), quarter)
         lhs = jnp.concatenate([hd[0, span, :], hd[1, span, :]], axis=1)
         part = pl.ds(half * (xs // 2), xs // 2)
-        rhs = jnp.concatenate(
-            [gw[1, p, part].reshape(d_model // 2, width) for p in range(4)], axis=1
+        source = (gd0, gd1)[j]
+        count = xs // 2 * zs * source.shape[3]
+        rhs = jnp.concatenate([source[p, part].reshape(count, width) for p in range(4)], axis=1)
+        return nt_dot(lhs, rhs)
+
+    def sums(j, k, half):
+        at_sem = j * 6 + 2 * k + half
+        return remote(
+            sb[j].at[k, half], rb[j].at[k, half], rs_send.at[at_sem], rs_recv.at[at_sem], (f, t_core)
         )
-        return nt_dot(lhs, rhs)
-
-    def sums(k, half, target):
-        return remote(
-            sb.at[k, half], rb.at[k, half], rs_send.at[2 * k + half], rs_recv.at[2 * k + half],
-            (f, target),
-        )
-
-    to_core = [sums(0, half, t_core) for half in (0, 1)]
-    far_sums = far_out([sb.at[1, half] for half in (0, 1)], rs_hop, 8)
-    far_sums_on = far_on(rs_hop, lambda q, half: rb.at[1, half], 8)
-    to_core2 = [sums(2, half, t_core) for half in (0, 1)]
-
+
+    sb, rb, acc, rs_hop = (sb0, sb1), (rb0, rb1), (acc0, acc1), (rs_hop0, rs_hop1)
+    to_core = [[sums(j, 0, half) for half in (0, 1)] for j in (0, 1)]
+    to_core2 = [[sums(j, 2, half) for half in (0, 1)] for j in (0, 1)]
+    far_sums = [far_out([sb[j].at[1, half] for half in (0, 1)], rs_hop[j], 8 + 4 * j) for j in (0, 1)]
+    far_sums_on = [
+        far_on(rs_hop[j], lambda q, half, j=j: rb[j].at[1, half], 8 + 4 * j) for j in (0, 1)
+    ]
+
+    def send_far(j):
+        for half in (0, 1):
+            sb[j][0, half] = partial(j, t_diag, half).astype(BF)
+            start([to_core[j][half]])
+        for half in (0, 1):
+            acc[j][half] = partial(j, t_far, half)
+            arrive([to_core[j][half]])
+            sb[j][1, half] = (acc[j][half] + rb[j][0, half].astype(F32)).astype(BF)
+            start([far_sums[j][half]])
+
+    def send_core(j):
+        for half in (0, 1):
+            sb[j][2, half] = partial(j, t_core, half).astype(BF)
+            start([to_core2[j][half]])
+        for half in (0, 1):
+            acc[j][half] = partial(j, t, half)
+
+    send_far(0)
+    last_a = advance(last_a, 2, 0, 1, 1)
+    send_core(0)
+    last_b = advance(last_b, 2, 1, 1, 1)
+    last_a = advance(last_a, 2, 0, 1, 2)
+    arrive(far_sums[0])
+    start(far_sums_on[0])
+    last_a = advance(last_a, 2, 0, 1, 3)
+    arrive(last_b[0] + last_b[1])
+    arrive(last_a[0] + last_a[1])
+    send_far(1)
+    send_core(1)
+    arrive(far_sums[1])
+    start(far_sums_on[1])
+
+    for j in (0, 1):
+        arrive(to_core2[j])
+        for half in (0, 1):
+            acc[j][half] = acc[j][half] + rb[j][2, half].astype(F32)
     for half in (0, 1):
-        sb[0, half] = partial(t_diag, half).astype(BF)
-        to_core[half].start()
-    for half in (0, 1):
-        acc[half] = partial(t_far, half)
-        to_core[half].wait_recv()
-        sb[1, half] = (acc[half] + rb[0, half].astype(F32)).astype(BF)
-        far_sums[half].start()
-    for half in (0, 1):
-        sb[2, half] = partial(t_core, half).astype(BF)
-        to_core2[half].start()
-    for half in (0, 1):
-        acc[half] = partial(t, half)
-    arrive(far_sums)
-    start(far_sums_on)
-    mine = pl.ds(pl.multiple_of(t * quarter, quarter), quarter)
-    for half in (0, 1):
-        to_core2[half].wait_recv()
-        far_sums_on[half].wait_recv()
+        deltas = []
+        for j in (0, 1):
+            arrive([far_sums_on[j][half]])
+            deltas.append(acc[j][half] + rb[j][1, half].astype(F32))
+        changed = (tp[half].astype(F32) + jnp.concatenate(deltas, axis=1)).astype(BF)
+        natural = nt_dot(changed, order_ref[...]).astype(BF)
         for k in (0, 1):
-            q = 2 * half + k
-            cols = slice(k * feat, (k + 1) * feat)
-            delta = acc[half, :, cols] + rb[2, half, :, cols].astype(F32) + rb[1, half, :, cols].astype(F32)
-            at[q] = (tk[q, mine, :].astype(F32) + delta).astype(BF)
+            at[2 * half + k] = natural[:, k * feat : (k + 1) * feat]
 
     at_copies = []
     for k in range(1, 4):
@@ -494,7 +551,7 @@
     fi_load.wait()
     fi_near.wait_recv()
     fi_relay.wait_recv()
-    for copy in loads:
+    for copy in loads[:-1]:
         copy.wait()
     pre = jnp.dot(
         jnp.concatenate([at[q] for q in range(4)], axis=1),
@@ -552,7 +609,7 @@
         for copy in high:
             copy.wait_send()
 
-    for copy in y_copies + done + tok_out + [tok_near] + at_copies + fx_copies + to_core + far_sums + to_core2:
+    for copy in y_copies + done + tok_out + [tok_near] + at_copies + fx_copies:
         copy.wait_send()
 
 
@@ -582,6 +639,8 @@
     grid_rows, grid_cols, chans = ocean_state.shape
     cells = grid_rows * grid_cols
     pick, place = halo_matrices(grid_rows, grid_cols)
+    order = order_matrix(2 * shard, xs * zs // 2)
+    parts = (xs * zs // 2 * FIRST, xs * zs // 2 * (2 * shard - FIRST))
     dma = pltpu.SemaphoreType.DMA
     vm = pl.BlockSpec(memory_space=pltpu.VMEM)
     hb = pl.BlockSpec(memory_space=pl.ANY)
@@ -591,24 +650,28 @@
             jax.ShapeDtypeStruct((rows, feat), BF),
             jax.ShapeDtypeStruct(ocean_state.shape, BF),
         ),
-        in_specs=[hb, vm, vm, vm, hb, hb, hb, vm, vm, hb, vm, vm, hb, hb, hb, hb],
+        in_specs=[hb, vm, vm, vm, hb, hb, hb, vm, vm, hb, vm, vm, hb, hb, hb, hb, hb],
         out_specs=(vm, vm),
         scratch_shapes=[
             pltpu.VMEM((2, shard, hidden), BF),
-            pltpu.VMEM((2, 4, xs, zs, 2 * shard, width), BF),
+            pltpu.VMEM((4, xs, zs, 2 * shard, width), BF),
+            pltpu.VMEM((4, xs, zs, FIRST, width), BF),
+            pltpu.VMEM((4, xs, zs, 2 * shard - FIRST, width), BF),
             pltpu.VMEM((4, rows, feat), BF),
             pltpu.VMEM((rows, d_model), BF),
             pltpu.VMEM((2, rows, hidden // 2), BF),
             pltpu.VMEM((4, feat, fh), BF),
-            pltpu.VMEM((3, 2, quarter, d_model // 2), BF),
-            pltpu.VMEM((3, 2, quarter, d_model // 2), BF),
-            pltpu.VMEM((2, quarter, d_model // 2), F32),
+            *(pltpu.VMEM((3, 2, quarter, n), BF) for n in parts),
+            *(pltpu.VMEM((3, 2, quarter, n), BF) for n in parts),
+            *(pltpu.VMEM((2, quarter, n), F32) for n in parts),
+            pltpu.VMEM((2, quarter, d_model // 2), BF),
+            pltpu.VMEM(order.shape, BF),
             pltpu.VMEM((4, quarter, feat), BF),
             pltpu.VMEM((4, quarter, feat), BF),
             pltpu.VMEM((6, quarter, flx), BF),
-            dma((2,)), dma((2,)), dma((128,)), dma((128,)),
+            dma((2,)), dma((2,)), dma((192,)), dma((192,)),
             dma((3,)), dma((3,)), dma((3,)), dma((3,)),
-            dma((6,)), dma((6,)), dma((3,)), dma((3,)),
+            dma((12,)), dma((12,)), dma((3,)), dma((3,)),
             dma((3,)), dma((3,)), dma((4,)), dma((2,)),
             pltpu.VMEM((cells, 128), F32),
             pltpu.VMEM((cells, 6 * quarter), BF),
@@ -628,11 +691,11 @@
             pltpu.VMEM(w_pw2.shape, BF),
             pltpu.VMEM(pick.shape, BF),
             pltpu.VMEM(place.shape, BF),
-            dma((9,)),
+            dma((10,)),
             pltpu.VMEM((2, rows // 2, feat), BF),
             pltpu.VMEM((2, feat // 2, fh), BF),
-            pltpu.VMEM((2, quarter, d_model // 2), BF),
-            dma((12,)), dma((12,)),
+            *(pltpu.VMEM((2, quarter, n), BF) for n in parts),
+            dma((16,)), dma((16,)),
         ],
         compiler_params=pltpu.CompilerParams(
             collective_id=0, has_side_effects=True, vmem_limit_bytes=60 * 1024 * 1024
@@ -641,7 +704,7 @@
     )(
         tokens, ln_gain, w_up, w_down.T, w_flux_in, w_flux_out,
         ocean_state, land_mask, column_map, w_couple, dw_kernel.transpose(1, 2, 0, 3), ocean_gain, w_pw1, w_pw2,
-        pick, place,
+        pick, place, order,
     )
 
 

time: 157 us -> 160 us (1.019)
  Pallas kernels: 154 us -> 156 us
    pallas_call x1, Pallas kernels: 154 us -> 156 us  [body(): pl.pallas_call(functools.partial(atmosphere_kernel, xs, zs), out_shape=(j...]
where the time goes in v5:
time: 160 us
  Pallas kernels  156 us (98%)
  local copies, waits for them, and re-layouts  2.95 us (2%)
    pallas_call x1, Pallas kernels, body(): pl.pallas_call(functools.partial(atmosphere_kernel, xs, zs), out_shape=(j...  156 us

profile of v5, /device:TPU:1, one launch (start us, length us, event | category | flops | bytes accessed | tf_op | source)
XLA Modules:
  0.0 160.0 jit_solution(3610360033022771580)
XLA Ops:
  0.6 156.4 %coupled_step.1 = (bf16[1024,384]{1,0:T(8,128)(2,1)}, bf16[32,32,256]{2,1,0:T(8,128)(2,1)}) custom-call(bf16[1024,384]{1,0:T(8,128)(2,1)} %tok_ref.1, f32[1536]{0:T(1024)} %gain_ref.1, bf16[24,1536]{1,0:T(8,128)(2,1)} %up_ref.1, bf16[24,1536]{1,0:T(8,128)(2,1)} %bitcast.3, bf16[384,768]{1,0:T(8,128)(2,1)} %wfi_ref.1, bf16[768,128]{1,0:T(8,128)(2,1)} %wfo_hbm.1, ...), custom_call_target="tpu_custom_call" | custom-call | tf_op jit(solution)/shard_map/coupled_step/pallas_call | solution.py:647
  157.0 0.0 copy-start
  157.0 2.1 %copy.21 = bf16[1024,384]{1,0:T(8,128)(2,1)} copy(bf16[1024,384]{1,0:T(8,128)(2,1)} %get-tuple-element.4) | data formatting | bytes 1572864
  159.2 0.0 copy-done
  159.2 0.8 copy.22
Async XLA Ops:
  157.0 2.2 %copy-start = (bf16[32,32,256]{2,1,0:T(8,128)(2,1)S(1)}, bf16[32,32,256]{2,1,0:T(8,128)(2,1)}, u32[]{:S(2)}) copy-start(bf16[32,32,256]{2,1,0:T(8,128)(2,1)} %get-tuple-element.5) | copy-start | bytes 1572868

commit v6 on v4

--- a/solution.py
+++ b/solution.py
@@ -370,25 +370,28 @@
     up_b = begin(0, 1)
     up_a = begin(0, 0)
     assemble(1, down_ref)
+    down_b = begin(1, 1)
+    down_a = begin(1, 0)
     up_a = advance(up_a, 0, 0, 0, 1)
     up_b = advance(up_b, 0, 1, 0, 1)
-    down_b = begin(1, 1)
+    down_b = advance(down_b, 1, 1, 0, 1)
+    down_a = advance(down_a, 1, 0, 0, 1)
     up_b = advance(up_b, 0, 1, 0, 2)
+    down_b = advance(down_b, 1, 1, 0, 2)
+    up_b = advance(up_b, 0, 1, 0, 3)
     up_a = advance(up_a, 0, 0, 1, 0)
+    down_b = advance(down_b, 1, 1, 0, 3)
+    up_b = advance(up_b, 0, 1, 1, 0)
     arrive(tok_out)
     start(tok_on)
-    up_b = advance(up_b, 0, 1, 0, 3)
-    down_a = begin(1, 0)
-    down_b = advance(down_b, 1, 1, 0, 1)
-    up_b = advance(up_b, 0, 1, 1, 0)
-    down_a = advance(down_a, 1, 0, 0, 1)
-    down_b = advance(down_b, 1, 1, 0, 2)
+    down_a = advance(down_a, 1, 0, 1, 0)
+    down_b = advance(down_b, 1, 1, 1, 0)
     up_a = advance(up_a, 0, 0, 1, 1)
     arrive(tok_on)
     start([tok_relay])
     start(fi_out)
     start([fi_near])
-    down_b = advance(down_b, 1, 1, 0, 3)
+    down_a = advance(down_a, 1, 0, 1, 1)
     tok_load.wait()
     tok_near.wait_recv()
     tok_relay.wait_recv()
@@ -406,17 +409,17 @@
             gain = gain_ref[q * feat : (q + 1) * feat][None, :]
             nm[span, q * feat : (q + 1) * feat] = (centers[q] * inverse * gain).astype(BF)
 
+    up_b = advance(up_b, 0, 1, 1, 1)
     up_a = advance(up_a, 0, 0, 1, 2)
-    up_b = advance(up_b, 0, 1, 1, 1)
+    down_b = advance(down_b, 1, 1, 1, 1)
+    down_a = advance(down_a, 1, 0, 1, 2)
     ocean_prepare(f * rows - quarter, mask_ref, map_ref, taps_ref, mk, oh, wb)
     up_a = advance(up_a, 0, 0, 1, 3)
-    down_a = advance(down_a, 1, 0, 1, 0)
+    down_a = advance(down_a, 1, 0, 1, 3)
     arrive(fi_out)
     start(fi_on)
     arrive(up_b[0] + up_b[1])
-    down_b = advance(down_b, 1, 1, 1, 0)
     arrive(up_a[0] + up_a[1])
-    down_a = advance(down_a, 1, 0, 1, 1)
 
     def up_block(half, block):
         span = pl.ds(pl.multiple_of(block * quarter, quarter), quarter)
@@ -432,11 +435,8 @@
             up_block(half, block)
 
         if half == 0:
-            down_a = advance(down_a, 1, 0, 1, 2)
-            down_b = advance(down_b, 1, 1, 1, 1)
             arrive(fi_on)
             start([fi_relay])
-    down_a = advance(down_a, 1, 0, 1, 3)
     arrive(down_b[0] + down_b[1])
     arrive(down_a[0] + down_a[1])
 

time: 157 us -> 155 us (0.987)
  Pallas kernels: 154 us -> 151 us
    pallas_call x1, Pallas kernels: 154 us -> 151 us  [body(): pl.pallas_call(functools.partial(atmosphere_kernel, xs, zs), out_shape=(j...]
where the time goes in v6:
time: 155 us; the launch traced here: 154 us
  Pallas kernels  151 us (97%)
  local copies, waits for them, and re-layouts  2.95 us (2%)
    pallas_call x1, Pallas kernels, body(): pl.pallas_call(functools.partial(atmosphere_kernel, xs, zs), out_shape=(j...  151 us

profile of v6, /device:TPU:1, one launch (start us, length us, event | category | flops | bytes accessed | tf_op | source)
XLA Modules:
  0.0 154.4 jit_solution(2545511562210124292)
XLA Ops:
  0.6 150.8 %coupled_step.1 = (bf16[1024,384]{1,0:T(8,128)(2,1)}, bf16[32,32,256]{2,1,0:T(8,128)(2,1)}) custom-call(bf16[1024,384]{1,0:T(8,128)(2,1)} %tok_ref.1, f32[1536]{0:T(1024)} %gain_ref.1, bf16[24,1536]{1,0:T(8,128)(2,1)} %up_ref.1, bf16[24,1536]{1,0:T(8,128)(2,1)} %bitcast.3, bf16[384,768]{1,0:T(8,128)(2,1)} %wfi_ref.1, bf16[768,128]{1,0:T(8,128)(2,1)} %wfo_hbm.1, ...), custom_call_target="tpu_custom_call" | custom-call | tf_op jit(solution)/shard_map/coupled_step/pallas_call | solution.py:588
  151.5 0.0 copy-start
  151.5 2.1 %copy.20 = bf16[1024,384]{1,0:T(8,128)(2,1)} copy(bf16[1024,384]{1,0:T(8,128)(2,1)} %get-tuple-element.4) | data formatting | bytes 1572864
  153.7 0.0 copy-done
  153.7 0.8 copy.21
Async XLA Ops:
  151.5 2.2 %copy-start = (bf16[32,32,256]{2,1,0:T(8,128)(2,1)S(1)}, bf16[32,32,256]{2,1,0:T(8,128)(2,1)}, u32[]{:S(2)}) copy-start(bf16[32,32,256]{2,1,0:T(8,128)(2,1)} %get-tuple-element.5) | copy-start | bytes 1572868

commit v7 on v6

--- a/solution.py
+++ b/solution.py
@@ -83,7 +83,6 @@
         keep(0, i, span, masked(span, before + forcing))
 
     for k in range(2):
-        pk[k] = jnp.dot(pick_ref[...], st[k], preferred_element_type=F32).astype(BF)
         last = grid_rows * grid_cols - edge
         moves = [
             (st.at[k, pl.ds(last, edge)], rn.at[k, 0], (f_next, t)),
@@ -101,7 +100,10 @@
             remote(src, dst, halo_send.at[k * 8 + j], halo_recv.at[k * 8 + j], device)
             for j, (src, dst, device) in enumerate(moves)
         ]
-        for copy in copies:
+        for copy in copies[:2]:
+            copy.start()
+        pk[k] = jnp.dot(pick_ref[...], st[k], preferred_element_type=F32).astype(BF)
+        for copy in copies[4:] + copies[2:4]:
             copy.start()
         for copy in copies:
             copy.wait_recv()
@@ -456,29 +458,39 @@
         )
 
     to_core = [sums(0, half, t_core) for half in (0, 1)]
-    far_sums = far_out([sb.at[1, half] for half in (0, 1)], rs_hop, 8)
-    far_sums_on = far_on(rs_hop, lambda q, half: rb.at[1, half], 8)
+    strip = quarter // 2
+    strips = [pl.ds(h * strip, strip) for h in (0, 1)]
+    far_sums = [
+        far_out([sb.at[1, half, part] for part in strips], rs_hop.at[half], 8 + 4 * half)
+        for half in (0, 1)
+    ]
+    far_sums_on = [
+        far_on(
+            rs_hop.at[half], lambda q, h, half=half: rb.at[1, half, strips[h]], 8 + 4 * half
+        )
+        for half in (0, 1)
+    ]
     to_core2 = [sums(2, half, t_core) for half in (0, 1)]
 
     for half in (0, 1):
         sb[0, half] = partial(t_diag, half).astype(BF)
         to_core[half].start()
-    for half in (0, 1):
         acc[half] = partial(t_far, half)
         to_core[half].wait_recv()
         sb[1, half] = (acc[half] + rb[0, half].astype(F32)).astype(BF)
-        far_sums[half].start()
+        start(far_sums[half])
     for half in (0, 1):
         sb[2, half] = partial(t_core, half).astype(BF)
         to_core2[half].start()
     for half in (0, 1):
         acc[half] = partial(t, half)
-    arrive(far_sums)
-    start(far_sums_on)
+    for half in (0, 1):
+        arrive(far_sums[half])
+        start(far_sums_on[half])
     mine = pl.ds(pl.multiple_of(t * quarter, quarter), quarter)
     for half in (0, 1):
         to_core2[half].wait_recv()
-        far_sums_on[half].wait_recv()
+        arrive(far_sums_on[half])
         for k in (0, 1):
             q = 2 * half + k
             cols = slice(k * feat, (k + 1) * feat)
@@ -552,7 +564,7 @@
         for copy in high:
             copy.wait_send()
 
-    for copy in y_copies + done + tok_out + [tok_near] + at_copies + fx_copies + to_core + far_sums + to_core2:
+    for copy in y_copies + done + tok_out + [tok_near] + at_copies + fx_copies + to_core + to_core2:
         copy.wait_send()
 
 
@@ -631,8 +643,8 @@
             dma((9,)),
             pltpu.VMEM((2, rows // 2, feat), BF),
             pltpu.VMEM((2, feat // 2, fh), BF),
-            pltpu.VMEM((2, quarter, d_model // 2), BF),
-            dma((12,)), dma((12,)),
+            pltpu.VMEM((2, 2, quarter // 2, d_model // 2), BF),
+            dma((16,)), dma((16,)),
         ],
         compiler_params=pltpu.CompilerParams(
             collective_id=0, has_side_effects=True, vmem_limit_bytes=60 * 1024 * 1024

time: 155 us -> 152 us (0.981)
  Pallas kernels: 151 us -> 148 us
    pallas_call x1, Pallas kernels: 151 us -> 148 us  [body(): pl.pallas_call(functools.partial(atmosphere_kernel, xs, zs), out_shape=(j...]
where the time goes in v7:
time: 152 us
  Pallas kernels  148 us (97%)
  local copies, waits for them, and re-layouts  2.95 us (2%)
    pallas_call x1, Pallas kernels, body(): pl.pallas_call(functools.partial(atmosphere_kernel, xs, zs), out_shape=(j...  148 us

profile of v7, /device:TPU:1, one launch (start us, length us, event | category | flops | bytes accessed | tf_op | source)
XLA Modules:
  0.0 151.7 jit_solution(15152116986223081189)
XLA Ops:
  0.6 148.1 %coupled_step.1 = (bf16[1024,384]{1,0:T(8,128)(2,1)}, bf16[32,32,256]{2,1,0:T(8,128)(2,1)}) custom-call(bf16[1024,384]{1,0:T(8,128)(2,1)} %tok_ref.1, f32[1536]{0:T(1024)} %gain_ref.1, bf16[24,1536]{1,0:T(8,128)(2,1)} %up_ref.1, bf16[24,1536]{1,0:T(8,128)(2,1)} %bitcast.3, bf16[384,768]{1,0:T(8,128)(2,1)} %wfi_ref.1, bf16[768,128]{1,0:T(8,128)(2,1)} %wfo_hbm.1, ...), custom_call_target="tpu_custom_call" | custom-call | tf_op jit(solution)/shard_map/coupled_step/pallas_call | solution.py:600
  148.7 0.0 copy-start
  148.8 2.1 %copy.20 = bf16[1024,384]{1,0:T(8,128)(2,1)} copy(bf16[1024,384]{1,0:T(8,128)(2,1)} %get-tuple-element.4) | data formatting | bytes 1572864
  150.9 0.0 copy-done
  150.9 0.8 copy.21
Async XLA Ops:
  148.7 2.2 %copy-start = (bf16[32,32,256]{2,1,0:T(8,128)(2,1)S(1)}, bf16[32,32,256]{2,1,0:T(8,128)(2,1)}, u32[]{:S(2)}) copy-start(bf16[32,32,256]{2,1,0:T(8,128)(2,1)} %get-tuple-element.5) | copy-start | bytes 1572868

commit v8 on v7

--- a/solution.py
+++ b/solution.py
@@ -81,6 +81,24 @@
         forcing = jnp.dot(picked, couple_ref[...], preferred_element_type=F32)
         before = sea_ref[pl.ds(i * 8, 8)].reshape(cells, chans).astype(F32)
         keep(0, i, span, masked(span, before + forcing))
+
+    halves = chans // 128
+
+    def correlate(k, quad, half, spans):
+        first = quad * 4
+        lanes = pl.ds(pl.multiple_of(half * 128, 128), 128)
+        totals = [[jnp.zeros((hi - lo, 8, 128), F32) for lo, hi in spans] for _ in range(4)]
+        for b in range(7):
+            weights = [wb[k, a, b, :, lanes] for a in range(7)]
+            for r in range(10):
+                for n, (lo, hi) in enumerate(spans):
+                    values = sh[b, first + r, lo:hi, :, lanes]
+                    for j in range(4):
+                        if 0 <= r - j < 7:
+                            totals[j][n] = totals[j][n] + values * weights[r - j]
+        for j in range(4):
+            for n, (lo, hi) in enumerate(spans):
+                cv[first + j, lo:hi, :, lanes] = totals[j][n]
 
     for k in range(2):
         last = grid_rows * grid_cols - edge
@@ -105,6 +123,19 @@
         pk[k] = jnp.dot(pick_ref[...], st[k], preferred_element_type=F32).astype(BF)
         for copy in copies[4:] + copies[2:4]:
             copy.start()
+
+        @pl.loop(3, grid_rows + 3)
+        def _(r):
+            line = pd[r, 8 : 8 + grid_cols, :]
+            for b in range(7):
+                sh[b, r, 1 : grid_cols // 8 - 1] = line[5 + b : 5 + b + grid_cols - 16].reshape(
+                    grid_cols // 8 - 2, 8, chans
+                )
+
+        @pl.loop(0, (grid_rows // 4 - 2) * halves)
+        def _(i):
+            correlate(k, 1 + i // halves, i % halves, ((1, grid_cols // 8 - 1),))
+
         for copy in copies:
             copy.wait_recv()
         if k == 0:
@@ -142,20 +173,17 @@
             for b in range(7):
                 sh[b, r] = line[5 + b : 5 + b + grid_cols].reshape(grid_cols // 8, 8, chans)
 
-        @pl.loop(0, (grid_rows // 4) * (chans // 128))
+        last_quad = grid_rows // 4 - 1
+        tiles = grid_cols // 8
+
+        @pl.loop(0, halves)
         def _(i):
-            first = (i // (chans // 128)) * 4
-            lanes = pl.ds(pl.multiple_of((i % (chans // 128)) * 128, 128), 128)
-            totals = [jnp.zeros((grid_cols // 8, 8, 128), F32) for _ in range(4)]
-            for b in range(7):
-                weights = [wb[k, a, b, :, lanes] for a in range(7)]
-                for r in range(10):
-                    values = sh[b, first + r, :, :, lanes]
-                    for j in range(4):
-                        if 0 <= r - j < 7:
-                            totals[j] = totals[j] + values * weights[r - j]
-            for j in range(4):
-                cv[first + j, :, :, lanes] = totals[j]
+            correlate(k, 0, i, ((0, tiles),))
+            correlate(k, last_quad, i, ((0, tiles),))
+
+        @pl.loop(0, (last_quad - 1) * halves)
+        def _(i):
+            correlate(k, 1 + i // halves, i % halves, ((0, 1), (tiles - 1, tiles)))
 
         @pl.loop(0, grid_rows // 8)
         def _(i):

time: 152 us -> 150 us (0.987)
  Pallas kernels: 148 us -> 146 us
    pallas_call x1, Pallas kernels: 148 us -> 146 us  [body(): pl.pallas_call(functools.partial(atmosphere_kernel, xs, zs), out_shape=(j...]
where the time goes in v8:
time: 150 us; the launch traced here: 149 us
  Pallas kernels  146 us (97%)
  local copies, waits for them, and re-layouts  2.95 us (2%)
    pallas_call x1, Pallas kernels, body(): pl.pallas_call(functools.partial(atmosphere_kernel, xs, zs), out_shape=(j...  146 us

profile of v8, /device:TPU:1, one launch (start us, length us, event | category | flops | bytes accessed | tf_op | source)
XLA Modules:
  0.0 149.4 jit_solution(1903121445733304192)
XLA Ops:
  0.6 145.8 %coupled_step.1 = (bf16[1024,384]{1,0:T(8,128)(2,1)}, bf16[32,32,256]{2,1,0:T(8,128)(2,1)}) custom-call(bf16[1024,384]{1,0:T(8,128)(2,1)} %tok_ref.1, f32[1536]{0:T(1024)} %gain_ref.1, bf16[24,1536]{1,0:T(8,128)(2,1)} %up_ref.1, bf16[24,1536]{1,0:T(8,128)(2,1)} %bitcast.3, bf16[384,768]{1,0:T(8,128)(2,1)} %wfi_ref.1, bf16[768,128]{1,0:T(8,128)(2,1)} %wfo_hbm.1, ...), custom_call_target="tpu_custom_call" | custom-call | tf_op jit(solution)/shard_map/coupled_step/pallas_call | solution.py:628
  146.4 0.0 copy-start
  146.4 2.1 %copy.20 = bf16[1024,384]{1,0:T(8,128)(2,1)} copy(bf16[1024,384]{1,0:T(8,128)(2,1)} %get-tuple-element.4) | data formatting | bytes 1572864
  148.6 0.0 copy-done
  148.6 0.8 copy.21
Async XLA Ops:
  146.4 2.2 %copy-start = (bf16[32,32,256]{2,1,0:T(8,128)(2,1)S(1)}, bf16[32,32,256]{2,1,0:T(8,128)(2,1)}, u32[]{:S(2)}) copy-start(bf16[32,32,256]{2,1,0:T(8,128)(2,1)} %get-tuple-element.5) | copy-start | bytes 1572868
